TPU v7x, 256 devices: a whole 4x4x8 slice. The times are simulated.
256 devices in a mesh: ev: 8 (over z), sp: 32 (over x, y, core).
Axes of the slice: x: 4, y: 4, z: 8, core: 2. Of those that a mesh axis runs over, the one named last changes fastest.
Arguments:
- kernels: bfloat16 [8, 3, 125, 32768], P('ev', None, None, 'sp'), may hold values from -6 to 6
- basis: bfloat16 [8, 125], replicated, may hold values from -0.5 to 0.5
- crossing: float32 [8, 4, 32768], P('ev', None, 'sp'), may hold values from 0.1 to 1
- owner: int32 [8, 4, 32768], P('ev', None, 'sp'), may hold values from 0 to 255, as said below
- target: int32 [8, 4, 32768], P('ev', None, 'sp'), may hold values from 0 to 8191
- diffusivity: float32 [32, 128, 512], P('ev', 'sp'), may hold values from 0.05 to 0.16
Outputs:
- smoothed: float32 [24, 32, 128, 512], P(None, 'ev', 'sp')
Inputs may be any that keep to these rules, and one draw needn't show every extreme that they name: `owner`: event slabs and inversion blocks are geometrically aligned: the 4 x 1024 slots of the elements in slab j (elements j * 1024 to (j + 1) * 1024 - 1) of an event name only blocks of columns j - 1, j and j + 1 (block b lies in column b % 32); they name any one block at most 256 times, and every block of column j exactly 256 times.
All inputs are finite; a program needn't handle non-finite values.
Results may differ from a plain program's by a relative error of at most 0.0003.
Values sent between devices are 32-bit elements; how exact they have to be, the bound alone decides.
A program may use at most 128 MiB of HBM per device.

v0:
```python
import jax
import jax.numpy as jnp
from jax import lax
from jax.sharding import PartitionSpec as P

STEPS = 4


def shifted(block, axis, distance):
    devices = range(lax.axis_size(axis))
    route = [(i - distance, i) for i in devices if i - distance in devices]
    return lax.ppermute(block, axis, route)


def with_halo(value, sides, width):
    for axis, dim in sides:
        size, length = (lax.axis_size(axis), value.shape[dim])
        up = [(i, (i + 1) % size) for i in range(size - 1)]
        down = [(j, i) for i, j in up]
        last = lax.slice_in_dim(value, length - width, length, axis=dim)
        initial = lax.slice_in_dim(value, 0, width, axis=dim)
        before = lax.ppermute(last, axis, up)
        after = lax.ppermute(initial, axis, down)
        value = jnp.concatenate([before, value, after], axis=dim)
    return value


def stencil(padded, coeff):
    zpadded = jnp.pad(padded, ((0, 0), (0, 0), (0, 0), (1, 1)))
    center = zpadded[:, 1:-1, 1:-1, 1:-1]
    total = zpadded[:, 2:, 1:-1, 1:-1] + zpadded[:, :-2, 1:-1, 1:-1]
    total = total + zpadded[:, 1:-1, 2:, 1:-1] + zpadded[:, 1:-1, :-2, 1:-1]
    total = total + zpadded[:, 1:-1, 1:-1, 2:] + zpadded[:, 1:-1, 1:-1, :-2]
    return center + coeff[None] * (total - 6.0 * center)


def per_device(kernels, basis, crossing, owner, target, diffusivity):
    count_ev = lax.axis_size("ev")
    count_sp = lax.axis_size("sp")
    column = lax.axis_index("sp")
    kernel_block = kernels[0]
    elements = kernel_block.shape[2]
    channels = kernel_block.shape[0] * basis.shape[0]
    projected = jnp.einsum("qg,pge->pqe", basis, kernel_block, preferred_element_type=jnp.float32)
    projected = projected.reshape(channels, elements)
    contribution = (projected[:, None, :] * crossing[0][None]).reshape(channels, -1)
    dest_flat = owner[0].reshape(-1)
    local_flat = target[0].reshape(-1)
    slots_total = dest_flat.shape[0]
    capacity = slots_total // (2 * count_ev)
    side = dest_flat % count_sp - column + 1
    bucket = side * count_ev + dest_flat // count_sp
    sort_order = jnp.argsort(bucket, stable=True)
    sorted_bucket = bucket[sort_order]
    counter = jnp.arange(slots_total, dtype=jnp.int32)
    is_first = jnp.concatenate([jnp.ones((1,), jnp.bool_), sorted_bucket[1:] != sorted_bucket[:-1]])
    group_start = lax.cummax(jnp.where(is_first, counter, 0), axis=0)
    position = sorted_bucket * capacity + (counter - group_start)
    send_values = jnp.zeros((channels, 3 * count_ev * capacity), jnp.float32)
    send_values = send_values.at[:, position].set(contribution[:, sort_order])
    send_cells = (
        jnp.zeros((3 * count_ev * capacity,), jnp.int32).at[position].set(local_flat[sort_order])
    )
    send_values = send_values.reshape(channels, 3, count_ev, capacity)
    send_cells = send_cells.reshape(1, 3, count_ev, capacity)
    from_left, cells_left = shifted((send_values[:, 2:3], send_cells[:, 2:3]), "sp", 1)
    from_right, cells_right = shifted((send_values[:, 0:1], send_cells[:, 0:1]), "sp", -1)
    column_values = jnp.concatenate([from_left, send_values[:, 1:2], from_right], axis=1)
    column_cells = jnp.concatenate([cells_left, send_cells[:, 1:2], cells_right], axis=1)
    cells_dev = diffusivity.shape[0] * diffusivity.shape[1] * diffusivity.shape[2]
    offsets = jnp.arange(count_ev, dtype=jnp.int32)[None, :, None] * cells_dev
    column_index = (column_cells[0] + offsets).reshape(-1)
    column_sum = jnp.zeros((channels, count_ev * cells_dev), jnp.float32)
    column_sum = column_sum.at[:, column_index].add(column_values.reshape(channels, -1))
    owned = lax.psum_scatter(
        column_sum.reshape(channels, count_ev, cells_dev), "ev", scatter_dimension=1, tiled=True
    )
    gradient = owned.reshape(channels, cells_dev)
    field = gradient.reshape(
        channels, diffusivity.shape[0], diffusivity.shape[1], diffusivity.shape[2]
    )
    for step in range(STEPS):
        padded = with_halo(field, (("ev", 1), ("sp", 2)), 1)
        field = stencil(padded, diffusivity)
    return field


def solution(mesh):
    return jax.shard_map(
        per_device,
        mesh=mesh,
        in_specs=(
            P("ev", None, None, "sp"),
            P(),
            P("ev", None, "sp"),
            P("ev", None, "sp"),
            P("ev", None, "sp"),
            P("ev", "sp", None),
        ),
        out_specs=P(None, "ev", "sp", None),
        check_vma=False,
    )
```

profile of v0, /device:TPU:6, one launch (start us, length us, event | category | flops | bytes accessed | tf_op | source)
XLA Modules:
  0.0 401.1 jit_solution(2923366297730778946)
XLA Ops:
  6.5 0.8 fusion.34
  7.4 5.8 %sort.17 = (s32[4096]{0:T(1024)}, s32[4096]{0:T(1024)S(1)}) sort(s32[4096]{0:T(1024)S(1)} %fusion.34, s32[4096]{0:T(1024)S(1)} %iota.26), dimensions={0}, to_apply=%region_0.1 | sort | flops 49152 | bytes 65536 | tf_op jit(solution)/shard_map/jit(argsort)/sort | solution.py:53
  13.2 23.0 %gather_fusion = s32[4096]{0:T(1024)S(1)} fusion(s32[4096]{0:T(1024)S(1)} %fusion.34, s32[4096]{0:T(1024)S(1)} %fusion.35), kind=kCustom, calls=%fused_computation | custom fusion | bytes 49152 | tf_op jit(solution)/shard_map/gather | solution.py:54
  36.3 23.0 %gather_fusion.1 = s32[4096]{0:T(1024)S(1)} fusion(s32[4096]{0:T(1024)S(1)} %bitcast.63, s32[4096]{0:T(1024)S(1)} %fusion.35), kind=kCustom, calls=%fused_computation.1 | custom fusion | bytes 49152 | tf_op jit(solution)/shard_map/gather | solution.py:62
  60.1 15.5 %scatter_custom_fusion = s32[6144]{0:T(1024)S(1)} fusion(s32[4096]{0:T(1024)S(1)} %bitcast.72, s32[4096]{0:T(1024)S(1)} %gather_fusion.1, s32[]{:T(128)} %constant.24.clone.1), kind=kCustom, calls=%fused_computation.128 | custom fusion | bytes 24580 | tf_op jit(solution)/shard_map/scatter | solution.py:62
  75.7 1.9 collective-permute-start
  77.6 5.8 %collective-permute-start.1 = (s32[1,1,8,256]{3,2,1,0:T(8,128)S(1)}, s32[1,1,8,256]{3,2,1,0:T(8,128)S(1)}, u32[]{:S(2)}, u32[]{:S(2)}) collective-permute-start(s32[1,1,8,256]{3,2,1,0:T(8,128)S(1)} %get-tuple-element.27), channel_id=1, source_target_pairs={{1,0},{2,1},{3,2},{4,3},{5,4},{6,5},{7,6},{8,7},{9,8},{10,9},{11,1... | collective-permute-start | bytes 24584 | tf_op jit(solution)/shard_map/ppermute | solution.py:12
  83.8 0.6 bitcast_multiply_fusion
  84.5 26.4 %scatter_custom_fusion.1 = f32[24,6144]{0,1:T(8,128)} fusion(s32[4096]{0:T(1024)S(1)} %bitcast.73, f32[24,4096]{0,1:T(8,128)S(1)} %bitcast_multiply_fusion, s32[4096]{0:T(1024)S(1)} %fusion.35, f32[]{:T(128)} %constant.23.clone.1), kind=kCustom, calls=%fused_computation.26 | custom fusion | bytes 589828 | tf_op jit(solution)/shard_map/scatter | solution.py:60
  110.9 3.1 fusion.44
  114.0 1.5 copy.50
  115.5 1.9 collective-permute-start.3
  117.5 0.3 copy.48
  117.8 2.9 collective-permute-start.2
  121.3 5.6 %collective-permute-done.2 = f32[24,1,8,256]{3,2,1,0:T(8,128)S(1)} collective-permute-done((f32[24,1,8,256]{3,2,1,0:T(8,128)S(1)}, f32[24,1,8,256]{3,2,1,0:T(8,128)S(1)}, u32[]{:S(2)}, u32[]{:S(2)}) %collective-permute-start.2) | collective-permute-done | bytes 196640 | tf_op jit(solution)/shard_map/ppermute | solution.py:12
  126.9 2.2 copy.47
  129.2 49.7 %scatter_custom_fusion.2 = f32[24,65536]{0,1:T(8,128)} fusion(s32[6144]{0:T(1024)S(1)} %bitcast.71, f32[6144,24]{1,0:T(8,128)} %bitcast.66, f32[]{:T(128)} %constant.23.clone.1), kind=kCustom, calls=%fused_computation.6 | custom fusion | flops 147456 | bytes 6291968 | tf_op jit(solution)/shard_map/scatter-add | solution.py:74
  178.9 20.0 %copy.22 = f32[24,8,8192]{2,0,1:T(8,128)} copy(f32[24,8,8192]{0,2,1:T(8,128)} %bitcast.64) | data formatting | bytes 12582912 | tf_op jit(solution)/shard_map/reshape | solution.py:76
  198.9 75.6 %reduce-scatter.2.cloned.1.call-done = f32[24,1,8192]{2,0,1:T(8,128)} async-done(((f32[24,8,8192]{2,0,1:T(8,128)}), f32[24,1,8192]{2,0,1:T(8,128)}) %reduce-scatter.2.cloned.1.call-update) | async-done | bytes 786448 | tf_op jit(solution)/shard_map/reduce_scatter | solution.py:75
  274.4 1.7 reshape_reshape.3
  276.1 1.7 collective-permute-start.5
  277.8 1.3 collective-permute-start.4
  279.1 2.9 collective-permute-done.5
  282.2 4.0 collective-permute-done.4
  286.2 0.5 fusion.45
  286.7 3.3 collective-permute-start.6
  290.1 2.1 collective-permute-start.7
  292.2 2.0 collective-permute-done.6
  294.5 5.7 %collective-permute-done.7 = f32[24,6,1,512]{3,0,2,1:T(8,128)S(1)} collective-permute-done((f32[24,6,1,512]{3,0,2,1:T(8,128)S(1)}, f32[24,6,1,512]{3,0,2,1:T(8,128)S(1)}, u32[]{:S(2)}, u32[]{:S(2)}) %collective-permute-start.7) | collective-permute-done | bytes 294944 | tf_op jit(solution)/shard_map/ppermute | solution.py:22
  300.5 2.7 select_maximum_fusion.12
  303.3 1.7 fusion.26
  305.0 4.8 %collective-permute-start.9 = (f32[24,1,4,512]{3,2,1,0:T(4,128)S(1)}, f32[24,1,4,512]{3,2,1,0:T(4,128)S(1)}, u32[]{:S(2)}, u32[]{:S(2)}) collective-permute-start(f32[24,1,4,512]{3,2,1,0:T(4,128)S(1)} %get-tuple-element.22), channel_id=1, source_target_pairs={{0,32},{32,64},{64,96},{96,128},{128,160},{160,192},{192,224},{1,3... | collective-permute-start | bytes 589832 | tf_op jit(solution)/shard_map/ppermute | solution.py:22
  309.8 1.3 collective-permute-start.8
  311.1 1.9 collective-permute-done.9
  312.9 4.4 %collective-permute-done.8 = f32[24,1,4,512]{3,2,1,0:T(4,128)S(1)} collective-permute-done((f32[24,1,4,512]{3,2,1,0:T(4,128)S(1)}, f32[24,1,4,512]{3,2,1,0:T(4,128)S(1)}, u32[]{:S(2)}, u32[]{:S(2)}) %collective-permute-start.8) | collective-permute-done | bytes 196640 | tf_op jit(solution)/shard_map/ppermute | solution.py:23
  317.4 0.5 pad_maximum_fusion.35
  317.9 1.9 collective-permute-start.10
  319.9 2.4 collective-permute-start.11
  322.3 1.7 collective-permute-done.10
  324.3 5.7 %collective-permute-done.11 = f32[24,6,1,512]{3,0,2,1:T(8,128)S(1)} collective-permute-done((f32[24,6,1,512]{3,0,2,1:T(8,128)S(1)}, f32[24,6,1,512]{3,0,2,1:T(8,128)S(1)}, u32[]{:S(2)}, u32[]{:S(2)}) %collective-permute-start.11) | collective-permute-done | bytes 294944 | tf_op jit(solution)/shard_map/ppermute | solution.py:22
  330.3 3.0 select_maximum_fusion.8
  333.4 1.8 fusion.20
  335.2 3.3 collective-permute-start.13
  338.5 1.3 collective-permute-start.12
  339.8 1.9 collective-permute-done.13
  341.7 4.4 %collective-permute-done.12 = f32[24,1,4,512]{3,2,1,0:T(4,128)S(1)} collective-permute-done((f32[24,1,4,512]{3,2,1,0:T(4,128)S(1)}, f32[24,1,4,512]{3,2,1,0:T(4,128)S(1)}, u32[]{:S(2)}, u32[]{:S(2)}) %collective-permute-start.12) | collective-permute-done | bytes 196640 | tf_op jit(solution)/shard_map/ppermute | solution.py:23
  346.1 0.5 pad_maximum_fusion.32
  346.6 2.3 collective-permute-start.14
  349.0 2.2 collective-permute-start.15
  351.2 1.9 collective-permute-done.14
  353.4 5.7 %collective-permute-done.15 = f32[24,6,1,512]{3,0,2,1:T(8,128)S(1)} collective-permute-done((f32[24,6,1,512]{3,0,2,1:T(8,128)S(1)}, f32[24,6,1,512]{3,0,2,1:T(8,128)S(1)}, u32[]{:S(2)}, u32[]{:S(2)}) %collective-permute-start.15) | collective-permute-done | bytes 294944 | tf_op jit(solution)/shard_map/ppermute | solution.py:22
  359.4 3.0 select_maximum_fusion.4
  362.5 1.8 fusion.14
  364.3 3.6 collective-permute-start.17
  367.9 1.3 collective-permute-start.16
  369.2 1.9 collective-permute-done.17
  371.1 4.4 %collective-permute-done.16 = f32[24,1,4,512]{3,2,1,0:T(4,128)S(1)} collective-permute-done((f32[24,1,4,512]{3,2,1,0:T(4,128)S(1)}, f32[24,1,4,512]{3,2,1,0:T(4,128)S(1)}, u32[]{:S(2)}, u32[]{:S(2)}) %collective-permute-start.16) | collective-permute-done | bytes 196640 | tf_op jit(solution)/shard_map/ppermute | solution.py:23
  375.5 0.5 pad_maximum_fusion.29
  376.0 1.9 collective-permute-start.18
  378.0 2.4 collective-permute-start.19
  380.4 1.7 collective-permute-done.18
  382.5 5.7 %collective-permute-done.19 = f32[24,6,1,512]{3,0,2,1:T(8,128)S(1)} collective-permute-done((f32[24,6,1,512]{3,0,2,1:T(8,128)S(1)}, f32[24,6,1,512]{3,0,2,1:T(8,128)S(1)}, u32[]{:S(2)}, u32[]{:S(2)}) %collective-permute-start.19) | collective-permute-done | bytes 294944 | tf_op jit(solution)/shard_map/ppermute | solution.py:22
  388.5 3.0 select_maximum_fusion
  391.5 2.5 fusion.8
  (65 shorter events, 5.0 us)
Async XLA Ops:
  6.5 76.9 %copy-start = (bf16[1,3,125,1024]{3,2,1,0:T(8,128)(2,1)S(1)}, bf16[1,3,125,1024]{3,2,1,0:T(8,128)(2,1)}, u32[]{:S(2)}) copy-start(bf16[1,3,125,1024]{3,2,1,0:T(8,128)(2,1)} %param.6) | copy-start | bytes 2304004
  6.5 267.9 %reduce-scatter.2.cloned.1.call-start = ((), (), s32[]{:S(2)}) async-start(), calls=%async_computation.1 | async-start | bytes 7077888 | tf_op jit(solution)/shard_map/reduce_scatter | solution.py:75
  13.1 23.1 %copy-start.3 = (s32[1,4,1024]{2,1,0:T(4,128)S(1)}, s32[1,4,1024]{2,1,0:T(4,128)}, u32[]{:S(2)}) copy-start(s32[1,4,1024]{2,1,0:T(4,128)} %param.10) | copy-start | bytes 49156
  36.3 47.1 %copy-start.4 = (f32[1,4,1024]{2,1,0:T(4,128)S(1)}, f32[1,4,1024]{2,1,0:T(4,128)}, u32[]{:S(2)}) copy-start(f32[1,4,1024]{2,1,0:T(4,128)} %param.8) | copy-start | bytes 49156
  36.3 47.1 %copy-start.5 = (bf16[8,125]{1,0:T(8,128)(2,1)S(1)}, bf16[8,125]{1,0:T(8,128)(2,1)}, u32[]{:S(2)}) copy-start(bf16[8,125]{1,0:T(8,128)(2,1)} %param.7) | copy-start | bytes 6004
  75.7 45.5 %collective-permute-start = (s32[1,1,8,256]{3,2,1,0:T(8,128)S(1)}, s32[1,1,8,256]{3,2,1,0:T(8,128)S(1)}, u32[]{:S(2)}, u32[]{:S(2)}) collective-permute-start(s32[1,1,8,256]{3,2,1,0:T(8,128)S(1)} %get-tuple-element.26), channel_id=1, source_target_pairs={{0,1},{1,2},{2,3},{3,4},{4,5},{5,6},{6,7},{7,8},{8,9},{9,10},{10,1... | collective-permute-start | bytes 24584 | tf_op jit(solution)/shard_map/ppermute | solution.py:12
  77.6 43.5 %collective-permute-start.1 = (s32[1,1,8,256]{3,2,1,0:T(8,128)S(1)}, s32[1,1,8,256]{3,2,1,0:T(8,128)S(1)}, u32[]{:S(2)}, u32[]{:S(2)}) collective-permute-start(s32[1,1,8,256]{3,2,1,0:T(8,128)S(1)} %get-tuple-element.27), channel_id=1, source_target_pairs={{1,0},{2,1},{3,2},{4,3},{5,4},{6,5},{7,6},{8,7},{9,8},{10,9},{11,1... | collective-permute-start | bytes 24584 | tf_op jit(solution)/shard_map/ppermute | solution.py:12
  115.5 5.7 %collective-permute-start.3 = (f32[24,1,8,256]{3,2,1,0:T(8,128)S(1)}, f32[24,1,8,256]{3,2,1,0:T(8,128)S(1)}, u32[]{:S(2)}, u32[]{:S(2)}) collective-permute-start(f32[24,1,8,256]{3,2,1,0:T(8,128)S(1)} %copy.50), channel_id=1, source_target_pairs={{1,0},{2,1},{3,2},{4,3},{5,4},{6,5},{7,6},{8,7},{9,8},{10,9},{11,1... | collective-permute-start | bytes 589832 | tf_op jit(solution)/shard_map/ppermute | solution.py:12
  117.8 9.1 %collective-permute-start.2 = (f32[24,1,8,256]{3,2,1,0:T(8,128)S(1)}, f32[24,1,8,256]{3,2,1,0:T(8,128)S(1)}, u32[]{:S(2)}, u32[]{:S(2)}) collective-permute-start(f32[24,1,8,256]{3,2,1,0:T(8,128)S(1)} %copy.48), channel_id=1, source_target_pairs={{0,1},{1,2},{2,3},{3,4},{4,5},{5,6},{6,7},{7,8},{8,9},{9,10},{10,1... | collective-permute-start | bytes 589832 | tf_op jit(solution)/shard_map/ppermute | solution.py:12
  276.1 5.9 %collective-permute-start.5 = (f32[24,1,4,512]{3,2,1,0:T(4,128)S(1)}, f32[24,1,4,512]{3,2,1,0:T(4,128)S(1)}, u32[]{:S(2)}, u32[]{:S(2)}) collective-permute-start(f32[24,1,4,512]{3,2,1,0:T(4,128)S(1)} %get-tuple-element.25), channel_id=1, source_target_pairs={{0,32},{32,64},{64,96},{96,128},{128,160},{160,192},{192,224},{1,3... | collective-permute-start | bytes 589832 | tf_op jit(solution)/shard_map/ppermute | solution.py:22
  277.8 8.3 %collective-permute-start.4 = (f32[24,1,4,512]{3,2,1,0:T(4,128)S(1)}, f32[24,1,4,512]{3,2,1,0:T(4,128)S(1)}, u32[]{:S(2)}, u32[]{:S(2)}) collective-permute-start(f32[24,1,4,512]{3,2,1,0:T(4,128)S(1)} %get-tuple-element.24), channel_id=1, source_target_pairs={{32,0},{64,32},{96,64},{128,96},{160,128},{192,160},{224,192},{33,... | collective-permute-start | bytes 589832 | tf_op jit(solution)/shard_map/ppermute | solution.py:23
  286.7 7.5 %collective-permute-start.6 = (f32[24,6,1,512]{3,0,2,1:T(8,128)S(1)}, f32[24,6,1,512]{3,0,2,1:T(8,128)S(1)}, u32[]{:S(2)}, u32[]{:S(2)}) collective-permute-start(f32[24,6,1,512]{3,0,2,1:T(8,128)S(1)} %copy.23), channel_id=1, source_target_pairs={{1,0},{2,1},{3,2},{4,3},{5,4},{6,5},{7,6},{8,7},{9,8},{10,9},{11,1... | collective-permute-start | bytes 884744 | tf_op jit(solution)/shard_map/ppermute | solution.py:23
  290.0 13.2 %copy-start.2 = (f32[4,4,512]{2,1,0:T(4,128)S(1)}, f32[4,4,512]{2,1,0:T(4,128)}, u32[]{:S(2)}) copy-start(f32[4,4,512]{2,1,0:T(4,128)} %param.11) | copy-start | bytes 98308
  290.1 10.2 %collective-permute-start.7 = (f32[24,6,1,512]{3,0,2,1:T(8,128)S(1)}, f32[24,6,1,512]{3,0,2,1:T(8,128)S(1)}, u32[]{:S(2)}, u32[]{:S(2)}) collective-permute-start(f32[24,6,1,512]{3,0,2,1:T(8,128)S(1)} %copy.25), channel_id=1, source_target_pairs={{0,1},{1,2},{2,3},{3,4},{4,5},{5,6},{6,7},{7,8},{8,9},{9,10},{10,1... | collective-permute-start | bytes 884744 | tf_op jit(solution)/shard_map/ppermute | solution.py:22
  305.0 8.0 %collective-permute-start.9 = (f32[24,1,4,512]{3,2,1,0:T(4,128)S(1)}, f32[24,1,4,512]{3,2,1,0:T(4,128)S(1)}, u32[]{:S(2)}, u32[]{:S(2)}) collective-permute-start(f32[24,1,4,512]{3,2,1,0:T(4,128)S(1)} %get-tuple-element.22), channel_id=1, source_target_pairs={{0,32},{32,64},{64,96},{96,128},{128,160},{160,192},{192,224},{1,3... | collective-permute-start | bytes 589832 | tf_op jit(solution)/shard_map/ppermute | solution.py:22
  309.8 7.6 %collective-permute-start.8 = (f32[24,1,4,512]{3,2,1,0:T(4,128)S(1)}, f32[24,1,4,512]{3,2,1,0:T(4,128)S(1)}, u32[]{:S(2)}, u32[]{:S(2)}) collective-permute-start(f32[24,1,4,512]{3,2,1,0:T(4,128)S(1)} %get-tuple-element.23), channel_id=1, source_target_pairs={{32,0},{64,32},{96,64},{128,96},{160,128},{192,160},{224,192},{33,... | collective-permute-start | bytes 589832 | tf_op jit(solution)/shard_map/ppermute | solution.py:23
  317.9 6.1 %collective-permute-start.10 = (f32[24,6,1,512]{3,0,2,1:T(8,128)S(1)}, f32[24,6,1,512]{3,0,2,1:T(8,128)S(1)}, u32[]{:S(2)}, u32[]{:S(2)}) collective-permute-start(f32[24,6,1,512]{3,0,2,1:T(8,128)S(1)} %copy.29), channel_id=1, source_target_pairs={{1,0},{2,1},{3,2},{4,3},{5,4},{6,5},{7,6},{8,7},{9,8},{10,9},{11,1... | collective-permute-start | bytes 884744 | tf_op jit(solution)/shard_map/ppermute | solution.py:23
  319.9 10.2 %collective-permute-start.11 = (f32[24,6,1,512]{3,0,2,1:T(8,128)S(1)}, f32[24,6,1,512]{3,0,2,1:T(8,128)S(1)}, u32[]{:S(2)}, u32[]{:S(2)}) collective-permute-start(f32[24,6,1,512]{3,0,2,1:T(8,128)S(1)} %copy.31), channel_id=1, source_target_pairs={{0,1},{1,2},{2,3},{3,4},{4,5},{5,6},{6,7},{7,8},{8,9},{9,10},{10,1... | collective-permute-start | bytes 884744 | tf_op jit(solution)/shard_map/ppermute | solution.py:22
  335.2 6.5 %collective-permute-start.13 = (f32[24,1,4,512]{3,2,1,0:T(4,128)S(1)}, f32[24,1,4,512]{3,2,1,0:T(4,128)S(1)}, u32[]{:S(2)}, u32[]{:S(2)}) collective-permute-start(f32[24,1,4,512]{3,2,1,0:T(4,128)S(1)} %get-tuple-element.20), channel_id=1, source_target_pairs={{0,32},{32,64},{64,96},{96,128},{128,160},{160,192},{192,224},{1,3... | collective-permute-start | bytes 589832 | tf_op jit(solution)/shard_map/ppermute | solution.py:22
  338.5 7.6 %collective-permute-start.12 = (f32[24,1,4,512]{3,2,1,0:T(4,128)S(1)}, f32[24,1,4,512]{3,2,1,0:T(4,128)S(1)}, u32[]{:S(2)}, u32[]{:S(2)}) collective-permute-start(f32[24,1,4,512]{3,2,1,0:T(4,128)S(1)} %get-tuple-element.21), channel_id=1, source_target_pairs={{32,0},{64,32},{96,64},{128,96},{160,128},{192,160},{224,192},{33,... | collective-permute-start | bytes 589832 | tf_op jit(solution)/shard_map/ppermute | solution.py:23
  346.6 6.5 %collective-permute-start.14 = (f32[24,6,1,512]{3,0,2,1:T(8,128)S(1)}, f32[24,6,1,512]{3,0,2,1:T(8,128)S(1)}, u32[]{:S(2)}, u32[]{:S(2)}) collective-permute-start(f32[24,6,1,512]{3,0,2,1:T(8,128)S(1)} %copy.35), channel_id=1, source_target_pairs={{1,0},{2,1},{3,2},{4,3},{5,4},{6,5},{7,6},{8,7},{9,8},{10,9},{11,1... | collective-permute-start | bytes 884744 | tf_op jit(solution)/shard_map/ppermute | solution.py:23
  349.0 10.2 %collective-permute-start.15 = (f32[24,6,1,512]{3,0,2,1:T(8,128)S(1)}, f32[24,6,1,512]{3,0,2,1:T(8,128)S(1)}, u32[]{:S(2)}, u32[]{:S(2)}) collective-permute-start(f32[24,6,1,512]{3,0,2,1:T(8,128)S(1)} %copy.37), channel_id=1, source_target_pairs={{0,1},{1,2},{2,3},{3,4},{4,5},{5,6},{6,7},{7,8},{8,9},{9,10},{10,1... | collective-permute-start | bytes 884744 | tf_op jit(solution)/shard_map/ppermute | solution.py:22
  364.3 6.8 %collective-permute-start.17 = (f32[24,1,4,512]{3,2,1,0:T(4,128)S(1)}, f32[24,1,4,512]{3,2,1,0:T(4,128)S(1)}, u32[]{:S(2)}, u32[]{:S(2)}) collective-permute-start(f32[24,1,4,512]{3,2,1,0:T(4,128)S(1)} %get-tuple-element.18), channel_id=1, source_target_pairs={{0,32},{32,64},{64,96},{96,128},{128,160},{160,192},{192,224},{1,3... | collective-permute-start | bytes 589832 | tf_op jit(solution)/shard_map/ppermute | solution.py:22
  367.9 7.6 %collective-permute-start.16 = (f32[24,1,4,512]{3,2,1,0:T(4,128)S(1)}, f32[24,1,4,512]{3,2,1,0:T(4,128)S(1)}, u32[]{:S(2)}, u32[]{:S(2)}) collective-permute-start(f32[24,1,4,512]{3,2,1,0:T(4,128)S(1)} %get-tuple-element.19), channel_id=1, source_target_pairs={{32,0},{64,32},{96,64},{128,96},{160,128},{192,160},{224,192},{33,... | collective-permute-start | bytes 589832 | tf_op jit(solution)/shard_map/ppermute | solution.py:23
  376.0 6.1 %collective-permute-start.18 = (f32[24,6,1,512]{3,0,2,1:T(8,128)S(1)}, f32[24,6,1,512]{3,0,2,1:T(8,128)S(1)}, u32[]{:S(2)}, u32[]{:S(2)}) collective-permute-start(f32[24,6,1,512]{3,0,2,1:T(8,128)S(1)} %copy.41), channel_id=1, source_target_pairs={{1,0},{2,1},{3,2},{4,3},{5,4},{6,5},{7,6},{8,7},{9,8},{10,9},{11,1... | collective-permute-start | bytes 884744 | tf_op jit(solution)/shard_map/ppermute | solution.py:23
  378.0 10.2 %collective-permute-start.19 = (f32[24,6,1,512]{3,0,2,1:T(8,128)S(1)}, f32[24,6,1,512]{3,0,2,1:T(8,128)S(1)}, u32[]{:S(2)}, u32[]{:S(2)}) collective-permute-start(f32[24,6,1,512]{3,0,2,1:T(8,128)S(1)} %copy.43), channel_id=1, source_target_pairs={{0,1},{1,2},{2,3},{3,4},{4,5},{5,6},{6,7},{7,8},{8,9},{9,10},{10,1... | collective-permute-start | bytes 884744 | tf_op jit(solution)/shard_map/ppermute | solution.py:22
  388.5 5.5 %copy-start.1 = (bf16[1,3,125,1024]{3,2,1,0:T(8,128)(2,1)S(1)}, bf16[1,3,125,1024]{3,2,1,0:T(8,128)(2,1)}, u32[]{:S(2)}) copy-start(bf16[1,3,125,1024]{3,2,1,0:T(8,128)(2,1)} %param.6) | copy-start | bytes 2304004
Sparse Core Ops, SparseCore 0:
  199.0 75.3 reduce-scatter.1
where the time goes:
time: 409 us; the launch traced here: 401 us
  waiting for transfers between devices  137 us (33%)
  local copies, waits for them, and re-layouts  121 us (30%)
  other arithmetic  78.5 us (19%)
  starting transfers between devices  49.6 us (12%)
  between operations  14.3 us (3%)
    reduce_scatter x1, waiting for transfers between devices, per_device(): lax.psum_scatter(column_sum.reshape(channels, count_ev, cells_dev), 'ev',...  75.6 us
    scatter-add x1, other arithmetic, per_device(): column_sum.at[:, column_index].add(column_values.reshape(channels, -1))  49.7 us
    ppermute x8, waiting for transfers between devices, with_halo(): before = lax.ppermute(last, axis, up)  31.2 us
    scatter x1, local copies, waits for them, and re-layouts, per_device(): send_values = send_values.at[:, position].set(contribution[:, sort_order])  26.4 us
    ppermute x8, waiting for transfers between devices, with_halo(): after = lax.ppermute(initial, axis, down)  24.6 us
    gather x1, local copies, waits for them, and re-layouts, per_device(): sorted_bucket = bucket[sort_order]  23 us
    gather x1, local copies, waits for them, and re-layouts, per_device(): local_flat[sort_order]  23 us
    ppermute x8, starting transfers between devices, with_halo(): before = lax.ppermute(last, axis, up)  22.6 us
  transfers between devices with their start and end apart: 21, of which 18 were waited for; matrix products, arithmetic and copies ran while one was open for 9% of the time, Pallas kernels for 0%

commit v1 on v0

v1 whole, which is shorter than its diff:
```python
import jax
import jax.numpy as jnp
from jax import lax
from jax.experimental import pallas as pl
from jax.experimental.pallas import tpu as pltpu
from jax.sharding import PartitionSpec as P

MESH = pl.DeviceIdType.MESH
STEPS = 4
F32 = jnp.float32
BF16 = jnp.bfloat16
NT = (((1,), (1,)), ((), ()))


def split(value):
    high = value.astype(BF16)
    low = (value - high.astype(F32)).astype(BF16)
    return high, low


def row_ids(rows, columns, group):
    return (lax.broadcasted_iota(jnp.int32, (rows, columns), 0) // group).astype(F32).astype(BF16)


def spread(ids, row, values):
    repeats = ids.shape[0] // values.shape[0]
    wide = jnp.broadcast_to(row.astype(BF16), ids.shape)
    tiled = jnp.concatenate([values] * repeats, axis=0)
    return jnp.where(ids == wide, tiled, jnp.zeros_like(tiled))


def kernel(n_ev, n_sp, kernels, basis, crossing, owner, target, diffusivity, out,
           value_send, cell_send, value_recv, cell_recv, field, halo,
           value_out_sem, cell_out_sem, value_in_sem, cell_in_sem, halo_out_sem, halo_in_sem):
    ev = lax.axis_index("ev")
    sp = lax.axis_index("sp")
    buckets = 3 * n_ev
    slots, elements = crossing.shape[1], crossing.shape[2]
    cap = value_send.shape[3]
    has = {0: sp > 0, 1: None, 2: sp < n_sp - 1}

    def when(condition, body):
        if condition is None:
            body()
        else:
            pl.when(condition)(body)

    def peer(bucket):
        return (lax.rem(ev + bucket // 3, n_ev), sp + bucket % 3 - 1)

    barrier = pltpu.get_barrier_semaphore()
    for bucket in range(buckets):
        if bucket == 1:
            continue

        def greet(bucket=bucket):
            pl.semaphore_signal(barrier, inc=1, device_id=peer(bucket), device_id_type=MESH)
        when(has[bucket % 3], greet)

    for side, missing in ((2, sp == 0), (0, sp == n_sp - 1)):
        @pl.when(missing)
        def _(side=side):
            for q in range(n_ev):
                value_recv[3 * q + side] = jnp.zeros(value_recv.shape[1:], F32)
                cell_recv[3 * q + side] = jnp.zeros(cell_recv.shape[1:], F32)
    for face, missing in enumerate((ev == 0, ev == n_ev - 1, sp == 0, sp == n_sp - 1)):
        @pl.when(missing)
        def _(face=face):
            for t in range(STEPS):
                halo[t, face] = jnp.zeros(halo.shape[2:], F32)

    projected = [
        lax.dot_general(basis[...], kernels[0, p], (((1,), (0,)), ((), ())), preferred_element_type=F32)
        for p in range(kernels.shape[1])
    ]

    owners = owner[0]
    row = lax.rem((owners >> 5) - ev + n_ev, n_ev)
    side = (owners & (n_sp - 1)) - sp + 1
    bucket_of = (row * 3 + side).astype(F32)
    chunk = 256
    per = elements // chunk
    ids32 = lax.broadcasted_iota(jnp.int32, (32, chunk), 0).astype(F32)
    hots = []
    for k in range(slots):
        for h in range(per):
            line = bucket_of[k:k + 1, h * chunk:(h + 1) * chunk]
            hots.append(jnp.where(ids32 == line, 1.0, 0.0))
    hot = jnp.concatenate(hots, axis=0).astype(BF16)
    ri = lax.broadcasted_iota(jnp.int32, (chunk, chunk), 0)
    ci = lax.broadcasted_iota(jnp.int32, (chunk, chunk), 1)
    before = jnp.where(ri < ci, 1.0, 0.0).astype(BF16)
    prefix = jnp.dot(hot, before, preferred_element_type=F32)
    total = jnp.dot(hot, jnp.ones((chunk, chunk), BF16), preferred_element_type=F32)
    carry = jnp.zeros((32, chunk), F32)
    rank_ids = row_ids(cap, chunk, 1)
    ranks = []
    for i in range(slots * per):
        rank = jnp.sum(hots[i] * (prefix[32 * i:32 * i + 32] + carry), axis=0, keepdims=True)
        carry = carry + total[32 * i:32 * i + 32]
        wide = jnp.broadcast_to(rank.astype(BF16), rank_ids.shape)
        ranks.append(jnp.where(rank_ids == wide, jnp.ones_like(wide), jnp.zeros_like(wide)))
    ids_b = row_ids(buckets * 8, elements, 8)
    ids_c = row_ids(32, elements, 1)
    sums = [None] * 4
    for k in range(slots):
        line = bucket_of[k:k + 1, :]
        hot_rank = jnp.concatenate(ranks[k * per:(k + 1) * per], axis=1)
        hot_rank = jnp.concatenate([hot_rank, hot_rank], axis=1)
        cells = target[0, k:k + 1, :]
        for g in range(4):
            if g < 3:
                high, low = split(projected[g] * crossing[0, k:k + 1, :])
                high = jnp.concatenate([high, high], axis=0)
                low = jnp.concatenate([low, low], axis=0)
                ids = ids_b
            else:
                high = jnp.broadcast_to((cells & -256).astype(F32).astype(BF16), (16, elements))
                low = jnp.broadcast_to((cells & 255).astype(F32).astype(BF16), (16, elements))
                ids = ids_c
            left = jnp.concatenate([spread(ids, line, high), spread(ids, line, low)], axis=1)
            part = lax.dot_general(left, hot_rank, NT, preferred_element_type=F32)
            sums[g] = part if k == 0 else sums[g] + part
    for g in range(3):
        value_send[:, g] = sums[g].reshape(buckets, 8, cap)
    cell_send[...] = sums[3][:buckets].reshape(buckets, 1, cap)

    pl.semaphore_wait(barrier, n_ev - 1 + n_ev * ((sp > 0).astype(jnp.int32) + (sp < n_sp - 1).astype(jnp.int32)))
    def move(bucket):
        return [
            pltpu.make_async_remote_copy(
                src_ref=source.at[bucket], dst_ref=dest.at[bucket], send_sem=out_sem.at[bucket],
                recv_sem=in_sem.at[bucket], device_id=peer(bucket), device_id_type=MESH)
            for source, dest, out_sem, in_sem in (
                (value_send, value_recv, value_out_sem, value_in_sem),
                (cell_send, cell_recv, cell_out_sem, cell_in_sem))
        ]
    order = [0] + [q for d in range(1, n_ev // 2) for q in (d, n_ev - d)] + [n_ev // 2]
    for q in order[::-1]:
        for s in range(3):
            if q == 0 and s == 1:
                continue

            def start(bucket=3 * q + s):
                for copy in move(bucket):
                    copy.start()
            when(has[s], start)
    value_recv[1] = value_send[1]
    cell_recv[1] = cell_send[1]

    field[0] = jnp.zeros(field.shape[1:], F32)
    ids_hi = row_ids(32 * 8, cap, 8)
    ids_lo = row_ids(256, cap, 1)
    for q in order:
        hot_lo = []
        lines = []
        for s in range(3):
            bucket = 3 * q + s
            if bucket != 1:
                def arrive(bucket=bucket):
                    for copy in move(bucket):
                        copy.wait_recv()
                when(has[2 - s], arrive)
            cells = cell_recv[bucket].astype(jnp.int32)
            wide = jnp.broadcast_to((cells & 255).astype(F32).astype(BF16), ids_lo.shape)
            hot_lo.append(jnp.where(ids_lo == wide, jnp.ones_like(wide), jnp.zeros_like(wide)))
            lines.append((cells >> 8).astype(F32))
        hot_lo = jnp.concatenate(hot_lo + hot_lo, axis=1)
        for g in range(3):
            highs, lows = [], []
            for s in range(3):
                high, low = split(value_recv[3 * q + s, g])
                high = jnp.concatenate([high, high], axis=0)
                low = jnp.concatenate([low, low], axis=0)
                highs.append(spread(ids_hi, lines[s], high))
                lows.append(spread(ids_hi, lines[s], low))
            left = jnp.concatenate(highs + lows, axis=1)
            part = lax.dot_general(left, hot_lo, NT, preferred_element_type=F32)
            part = part.reshape(4, 4, 2, 8, 256)
            for z in range(2):
                field[0, g, :, :, :, z * 256:(z + 1) * 256] += part[:, :, z]

    faces = (
        (ev < n_ev - 1, ev > 0, (ev + 1, sp), lambda t, g: field.at[t, g, 3]),
        (ev > 0, ev < n_ev - 1, (ev - 1, sp), lambda t, g: field.at[t, g, 0]),
        (sp < n_sp - 1, sp > 0, (ev, sp + 1), lambda t, g: field.at[t, g, :, 3]),
        (sp > 0, sp < n_sp - 1, (ev, sp - 1), lambda t, g: field.at[t, g, :, 0]),
    )
    def face_copy(t, g, face):
        _, _, device, source = faces[face]
        return pltpu.make_async_remote_copy(
            src_ref=source(t, g), dst_ref=halo.at[t, face, g], send_sem=halo_out_sem.at[t, face, g],
            recv_sem=halo_in_sem.at[t, face, g], device_id=device, device_id_type=MESH)

    def send_faces(t, g):
        for face in range(4):
            when(faces[face][0], lambda face=face: face_copy(t, g, face).start())
    lane = lax.broadcasted_iota(jnp.int32, (32, 512), 1)
    for g in range(3):
        send_faces(0, g)
    for t in range(STEPS):
        for g in range(3):
            for face in range(4):
                when(faces[face][1], lambda face=face: face_copy(t, g, face).wait_recv())
            for a in range(4):
                center = field[t, g, a]
                above = halo[t, 0, g] if a == 0 else field[t, g, a - 1]
                below = halo[t, 1, g] if a == 3 else field[t, g, a + 1]
                around = above + below
                around += jnp.concatenate([halo[t, 2, g, a][None], center[:3]], axis=0)
                around += jnp.concatenate([center[1:], halo[t, 3, g, a][None]], axis=0)
                flat = center.reshape(32, 512)
                left = jnp.where(lane == 0, 0.0, pltpu.roll(flat, 1, 1))
                right = jnp.where(lane == 511, 0.0, pltpu.roll(flat, 511, 1))
                around += (left + right).reshape(4, 8, 512)
                coeff = diffusivity[a].reshape(4, 1, 512)
                new = center + coeff * (around - 6.0 * center)
                if t < STEPS - 1:
                    field[t + 1, g, a] = new
                else:
                    out[g, a] = new
            if t < STEPS - 1:
                send_faces(t + 1, g)

    for q in range(n_ev):
        for s in range(3):
            if q == 0 and s == 1:
                continue

            def finish(bucket=3 * q + s):
                for copy in move(bucket):
                    copy.wait_send()
            when(has[s], finish)
    for t in range(STEPS):
        for g in range(3):
            for face in range(4):
                when(faces[face][0], lambda face=face: face_copy(t, g, face).wait_send())


def solution(mesh):
    n_ev, n_sp = mesh.shape["ev"], mesh.shape["sp"]

    def per_device(kernels, basis, crossing, owner, target, diffusivity):
        import functools
        buckets = 3 * n_ev
        cap = crossing.shape[1] * crossing.shape[2] // (2 * n_ev)
        result = pl.pallas_call(
            functools.partial(kernel, n_ev, n_sp),
            out_shape=jax.ShapeDtypeStruct((3, 4, 4, 8, 512), F32),
            in_specs=[pl.BlockSpec(memory_space=pltpu.VMEM)] * 6,
            out_specs=pl.BlockSpec(memory_space=pltpu.VMEM),
            scratch_shapes=[
                pltpu.VMEM((buckets, 3, 8, cap), F32),
                pltpu.VMEM((buckets, 1, cap), F32),
                pltpu.VMEM((buckets, 3, 8, cap), F32),
                pltpu.VMEM((buckets, 1, cap), F32),
                pltpu.VMEM((STEPS, 3, 4, 4, 8, 512), F32),
                pltpu.VMEM((STEPS, 4, 3, 4, 8, 512), F32),
                pltpu.SemaphoreType.DMA((buckets,)),
                pltpu.SemaphoreType.DMA((buckets,)),
                pltpu.SemaphoreType.DMA((buckets,)),
                pltpu.SemaphoreType.DMA((buckets,)),
                pltpu.SemaphoreType.DMA((STEPS, 4, 3)),
                pltpu.SemaphoreType.DMA((STEPS, 4, 3)),
            ],
            compiler_params=pltpu.CompilerParams(
                collective_id=0, has_side_effects=True, vmem_limit_bytes=48 * 1024 * 1024),
        )(kernels, basis, crossing, owner, target, diffusivity)
        result = result.transpose(0, 3, 1, 2, 4)
        return result.reshape(24, 4, 4, 512)

    return jax.shard_map(
        per_device,
        mesh=mesh,
        in_specs=(
            P("ev", None, None, "sp"),
            P(),
            P("ev", None, "sp"),
            P("ev", None, "sp"),
            P("ev", None, "sp"),
            P("ev", "sp", None),
        ),
        out_specs=P(None, "ev", "sp", None),
        check_vma=False,
    )
```

time: 409 us -> 62.2 us (0.15); the launches traced: 401 us -> 61.8 us
  waiting for transfers between devices: 137 us -> 0 us
  local copies, waits for them, and re-layouts: 121 us -> 6.16 us
  other arithmetic: 78.5 us -> 0 us
  Pallas kernels: 0 us -> 55.6 us
  starting transfers between devices: 49.6 us -> 0 us
  between operations: 14.3 us -> 0.02 us
    reduce_scatter x1 -> x0, waiting for transfers between devices: 75.6 us -> none  [per_device(): lax.psum_scatter(column_sum.reshape(channels, count_ev, cells_dev), 'ev',...]
    ppermute x20 -> x0, waiting for transfers between devices: 61.5 us -> none  [the longest x8 31.2 us: with_halo(): before = lax.ppermute(last, axis, up)]
    pallas_call x0 -> x1, Pallas kernels: none -> 55.6 us  [per_device(): pl.pallas_call(functools.partial(kernel, n_ev, n_sp), out_shape=jax.Shape...]
    scatter-add x1 -> x0, other arithmetic: 49.7 us -> none  [per_device(): column_sum.at[:, column_index].add(column_values.reshape(channels, -1))]
    ppermute x20 -> x0, starting transfers between devices: 49.6 us -> none  [the longest x8 22.6 us: with_halo(): before = lax.ppermute(last, axis, up)]
    gather x2 -> x0, local copies, waits for them, and re-layouts: 46.1 us -> none  [the longest x1 23 us: per_device(): sorted_bucket = bucket[sort_order]]
    scatter x2 -> x0, local copies, waits for them, and re-layouts: 42 us -> none  [the longest x1 26.4 us: per_device(): send_values = send_values.at[:, position].set(contribution[:, sort_order])]
    reshape x3 -> x2, local copies, waits for them, and re-layouts: 22.2 us -> 1.44 us  [per_device(): return result.reshape(24, 4, 4, 512)]
  transfers between devices with their start and end apart: 21 -> 0, of which waited for: 18 -> 0; matrix products, arithmetic and copies ran while one was open for 9% -> 0% of each run, Pallas kernels for 0% -> 0%
where the time goes in v1:
time: 62.2 us; the launch traced here: 61.8 us
  Pallas kernels  55.6 us (89%)
  local copies, waits for them, and re-layouts  6.16 us (10%)
    pallas_call x1, Pallas kernels, per_device(): pl.pallas_call(functools.partial(kernel, n_ev, n_sp), out_shape=jax.Shape...  55.6 us
    unnamed x12, local copies, waits for them, and re-layouts  4.72 us
    reshape x2, local copies, waits for them, and re-layouts, per_device(): return result.reshape(24, 4, 4, 512)  1.44 us

profile of v1, /device:TPU:6, one launch (start us, length us, event | category | flops | bytes accessed | tf_op | source)
XLA Modules:
  0.0 61.8 jit_solution(3529887637083937064)
XLA Ops:
  0.0 0.0 copy-start
  0.0 1.1 %copy-done = bf16[1,3,125,1024]{3,2,1,0:T(8,128)(2,1)S(1)} copy-done((bf16[1,3,125,1024]{3,2,1,0:T(8,128)(2,1)S(1)}, bf16[1,3,125,1024]{3,2,1,0:T(8,128)(2,1)}, u32[]{:S(2)}) %copy-start) | copy-done | bytes 768024
  1.1 0.0 copy-start.1
  1.1 0.8 %copy-done.1 = f32[4,4,512]{2,1,0:T(4,128)S(1)} copy-done((f32[4,4,512]{2,1,0:T(4,128)S(1)}, f32[4,4,512]{2,1,0:T(4,128)}, u32[]{:S(2)}) %copy-start.1) | copy-done | bytes 32792
  1.9 0.0 copy-start.2
  1.9 0.7 %copy-done.2 = f32[1,4,1024]{2,1,0:T(4,128)S(1)} copy-done((f32[1,4,1024]{2,1,0:T(4,128)S(1)}, f32[1,4,1024]{2,1,0:T(4,128)}, u32[]{:S(2)}) %copy-start.2) | copy-done | bytes 16408
  2.6 0.0 copy-start.3
  2.6 0.7 %copy-done.3 = s32[1,4,1024]{2,1,0:T(4,128)S(1)} copy-done((s32[1,4,1024]{2,1,0:T(4,128)S(1)}, s32[1,4,1024]{2,1,0:T(4,128)}, u32[]{:S(2)}) %copy-start.3) | copy-done | bytes 16408
  3.3 0.0 copy-start.4
  3.3 0.7 %copy-done.4 = s32[1,4,1024]{2,1,0:T(4,128)S(1)} copy-done((s32[1,4,1024]{2,1,0:T(4,128)S(1)}, s32[1,4,1024]{2,1,0:T(4,128)}, u32[]{:S(2)}) %copy-start.4) | copy-done | bytes 16408
  4.0 0.0 copy-start.5
  4.0 0.7 %copy-done.5 = bf16[8,125]{1,0:T(8,128)(2,1)S(1)} copy-done((bf16[8,125]{1,0:T(8,128)(2,1)S(1)}, bf16[8,125]{1,0:T(8,128)(2,1)}, u32[]{:S(2)}) %copy-start.5) | copy-done | bytes 2024
  4.7 55.6 %shard_map.64 = f32[3,4,4,8,512]{4,3,2,1,0:T(8,128)S(1)} custom-call(bf16[1,3,125,1024]{3,2,1,0:T(8,128)(2,1)S(1)} %copy-done, bf16[8,125]{1,0:T(8,128)(2,1)S(1)} %copy-done.5, f32[1,4,1024]{2,1,0:T(4,128)S(1)} %copy-done.2, s32[1,4,1024]{2,1,0:T(4,128)S(1)} %copy-done.3, s32[1,4,1024]{2,1,0:T(4,128)S(1)} %copy-done.4, f32[4,4,512]{2,1,0:T(4,128)S(1)} %copy-done.1), custom_call_target="tpu_custom_call" | custom-call | tf_op jit(solution)/shard_map/pallas_call | solution.py:247
  60.4 0.1 copy_bitcast_fusion
  60.4 1.4 %copy.8 = f32[24,4,4,512]{3,2,1,0:T(4,128)} copy(f32[24,4,4,512]{3,0,2,1:T(8,128)S(1)} %copy_bitcast_fusion) | data formatting | bytes 1572864 | tf_op jit(solution)/shard_map/reshape | solution.py:270
Async XLA Ops:
  0.0 1.1 %copy-start = (bf16[1,3,125,1024]{3,2,1,0:T(8,128)(2,1)S(1)}, bf16[1,3,125,1024]{3,2,1,0:T(8,128)(2,1)}, u32[]{:S(2)}) copy-start(bf16[1,3,125,1024]{3,2,1,0:T(8,128)(2,1)} %kernels.1) | copy-start | bytes 2304004
  1.1 0.8 %copy-start.1 = (f32[4,4,512]{2,1,0:T(4,128)S(1)}, f32[4,4,512]{2,1,0:T(4,128)}, u32[]{:S(2)}) copy-start(f32[4,4,512]{2,1,0:T(4,128)} %diffusivity.1) | copy-start | bytes 98308
  1.9 0.7 %copy-start.2 = (f32[1,4,1024]{2,1,0:T(4,128)S(1)}, f32[1,4,1024]{2,1,0:T(4,128)}, u32[]{:S(2)}) copy-start(f32[1,4,1024]{2,1,0:T(4,128)} %crossing.1) | copy-start | bytes 49156
  2.6 0.7 %copy-start.3 = (s32[1,4,1024]{2,1,0:T(4,128)S(1)}, s32[1,4,1024]{2,1,0:T(4,128)}, u32[]{:S(2)}) copy-start(s32[1,4,1024]{2,1,0:T(4,128)} %owner.1) | copy-start | bytes 49156
  3.3 0.7 %copy-start.4 = (s32[1,4,1024]{2,1,0:T(4,128)S(1)}, s32[1,4,1024]{2,1,0:T(4,128)}, u32[]{:S(2)}) copy-start(s32[1,4,1024]{2,1,0:T(4,128)} %target.1) | copy-start | bytes 49156
  4.0 0.7 %copy-start.5 = (bf16[8,125]{1,0:T(8,128)(2,1)S(1)}, bf16[8,125]{1,0:T(8,128)(2,1)}, u32[]{:S(2)}) copy-start(bf16[8,125]{1,0:T(8,128)(2,1)} %basis.1) | copy-start | bytes 6004

commit v2 on v1

v2 whole, which is shorter than its diff:
```python
import functools

import jax
import jax.numpy as jnp
from jax import lax
from jax.experimental import pallas as pl
from jax.experimental.pallas import tpu as pltpu
from jax.sharding import PartitionSpec as P

MESH = pl.DeviceIdType.MESH
STEPS = 4
PIECES = 4
F32 = jnp.float32
BF16 = jnp.bfloat16
NN = (((1,), (0,)), ((), ()))
NT = (((1,), (1,)), ((), ()))


def split(value):
    high = value.astype(BF16)
    low = (value - high.astype(F32)).astype(BF16)
    return high, low


def twice(value):
    return jnp.concatenate([value, value], axis=0)


def row_ids(rows, columns, group):
    return (lax.broadcasted_iota(jnp.int32, (rows, columns), 0) // group).astype(F32).astype(BF16)


def spread(ids, row, values):
    repeats = ids.shape[0] // values.shape[0]
    wide = jnp.broadcast_to(row.astype(BF16), ids.shape)
    tiled = jnp.concatenate([values] * repeats, axis=0)
    return jnp.where(ids == wide, tiled, jnp.zeros_like(tiled))


def one_hot(ids, row):
    wide = jnp.broadcast_to(row.astype(BF16), ids.shape)
    return jnp.where(ids == wide, jnp.ones_like(wide), jnp.zeros_like(wide))


def when(condition, body):
    if condition is None:
        body()
    else:
        pl.when(condition)(body)


def kernel(n_ev, n_sp, *refs):
    sources, out, inputs, input_sem = refs[:6], refs[6], refs[7:13], refs[13]
    loads = [pltpu.make_async_copy(sources[i], inputs[i], input_sem.at[i]) for i in range(6)]
    for i in (1, 0, 3, 4, 2, 5):
        loads[i].start()
    body(n_ev, n_sp, loads, *inputs, out, *refs[14:])


def body(n_ev, n_sp, loads, kernels, basis, crossing, owner, target, diffusivity, out,
         raw, lists, side_lists, field, halo,
         ring_out_sem, ring_in_sem, side_out_sem, side_in_sem, list_out_sem, list_in_sem,
         side_list_out_sem, side_list_in_sem,
         halo_out_sem, halo_in_sem):
    ev = lax.axis_index("ev")
    sp = lax.axis_index("sp")
    buckets = 3 * n_ev
    slots, elements = crossing.shape[1], crossing.shape[2]
    cap = lists.shape[5]
    piece = elements // PIECES
    half = n_ev // 2
    has = {0: sp > 0, 1: None, 2: sp < n_sp - 1}

    def beside(s):
        return (ev, sp + s - 1)

    def along(up):
        return (lax.rem(ev + (1 if up else n_ev - 1), n_ev), sp)

    barrier = pltpu.get_barrier_semaphore()
    for up in (True, False):
        pl.semaphore_signal(barrier, inc=1, device_id=along(up), device_id_type=MESH)
    for s in (0, 2):
        when(has[s], lambda s=s: pl.semaphore_signal(barrier, inc=1, device_id=beside(s), device_id_type=MESH))

    for s, missing in ((2, sp == 0), (0, sp == n_sp - 1)):
        @pl.when(missing)
        def _(s=s):
            raw[2 - s] = jnp.zeros(raw.shape[1:], F32)
            side_lists[s // 2] = jnp.zeros(side_lists.shape[1:], F32)
    for face, missing in enumerate((ev == 0, ev == n_ev - 1, sp == 0, sp == n_sp - 1)):
        @pl.when(missing)
        def _(face=face):
            for t in range(STEPS):
                halo[t, face] = jnp.zeros(halo.shape[2:], F32)

    loads[1].wait()
    loads[0].wait()
    for p in range(kernels.shape[1]):
        part = lax.dot_general(basis[...], kernels[0, p], NN, preferred_element_type=F32)
        for h in range(PIECES):
            raw[1, 0, h, 8 * p:8 * p + 8] = part[:, h * piece:(h + 1) * piece]

    def ring(q, h, up):
        to = (q + 1 if up else q - 1) % n_ev
        return pltpu.make_async_remote_copy(
            src_ref=raw.at[1, q, h], dst_ref=raw.at[1, to, h], send_sem=ring_out_sem.at[int(up), q, h],
            recv_sem=ring_in_sem.at[to, h], device_id=along(up), device_id_type=MESH)

    def ring_pieces(q, up):
        last = half - 1 if up else half + 1
        if q == half or (q != 0 and up != (q < half)):
            return ()
        if q != last:
            return range(PIECES)
        return range(PIECES // 2) if up else range(PIECES // 2, PIECES)

    def sideways(q, s):
        return pltpu.make_async_remote_copy(
            src_ref=raw.at[1, q], dst_ref=raw.at[2 - s, q], send_sem=side_out_sem.at[s // 2, q],
            recv_sem=side_in_sem.at[s // 2, q], device_id=beside(s), device_id_type=MESH)

    def arrive(places):
        for h in range(PIECES):
            for q in places:
                up = q < half
                if q == half:
                    up = h < PIECES // 2
                ring((q - 1 if up else q + 1) % n_ev, h, up).wait_recv()
                if h in ring_pieces(q, up):
                    ring(q, h, up).start()
        for q in places:
            for s in (0, 2):
                when(has[s], lambda q=q, s=s: sideways(q, s).start())

    def pass_lists(q, up):
        to = (q + 1 if up else q - 1) % n_ev
        rows = pl.ds(q + 1, half - q) if up else pl.ds(half + 1, (q or n_ev) - half - 1)
        return pltpu.make_async_remote_copy(
            src_ref=lists.at[q, rows], dst_ref=lists.at[to, rows], send_sem=list_out_sem.at[int(up), q],
            recv_sem=list_in_sem.at[to], device_id=along(up), device_id_type=MESH)

    def pass_lists_to(q):
        return [up for up in (True, False) if (q == 0) or (q < half if up else q > half + 1) and up == (q < half)]

    def lists_sideways(q, s):
        return pltpu.make_async_remote_copy(
            src_ref=lists.at[q, q, s], dst_ref=side_lists.at[s // 2, q], send_sem=side_list_out_sem.at[s // 2, q],
            recv_sem=side_list_in_sem.at[s // 2, q], device_id=beside(s), device_id_type=MESH)

    def arrive_lists(places):
        for q in places:
            up = q <= half
            if q != 0:
                pass_lists((q - 1 if up else q + 1) % n_ev, up).wait_recv()
            for up in pass_lists_to(q):
                pass_lists(q, up).start()
        for q in places:
            for s in (0, 2):
                when(has[s], lambda q=q, s=s: lists_sideways(q, s).start())

    pl.semaphore_wait(barrier, 2 + (sp > 0).astype(jnp.int32) + (sp < n_sp - 1).astype(jnp.int32))
    for h in range(PIECES):
        for up in (True, False):
            ring(0, h, up).start()
    for s in (0, 2):
        when(has[s], lambda s=s: sideways(0, s).start())

    loads[3].wait()
    owners = owner[0]
    row = lax.rem((owners >> 5) - ev + n_ev, n_ev)
    side = (owners & (n_sp - 1)) - sp + 1
    bucket_of = (row * 3 + side).astype(F32)
    chunk = 256
    per = elements // chunk
    ids_f32 = lax.broadcasted_iota(jnp.int32, (32, chunk), 0).astype(F32)
    hots = []
    for k in range(slots):
        for h in range(per):
            line = bucket_of[k:k + 1, h * chunk:(h + 1) * chunk]
            hots.append(jnp.where(ids_f32 == line, 1.0, 0.0))
    hot = jnp.concatenate(hots, axis=0).astype(BF16)
    ri = lax.broadcasted_iota(jnp.int32, (chunk, chunk), 0)
    ci = lax.broadcasted_iota(jnp.int32, (chunk, chunk), 1)
    before = jnp.where(ri < ci, 1.0, 0.0).astype(BF16)
    prefix = jnp.dot(hot, before, preferred_element_type=F32)
    total = jnp.dot(hot, jnp.ones((chunk, chunk), BF16), preferred_element_type=F32)
    carry = jnp.zeros((32, chunk), F32)
    ids_cap = row_ids(cap, chunk, 1)
    ranks = []
    for i in range(slots * per):
        rank = jnp.sum(hots[i] * (prefix[32 * i:32 * i + 32] + carry), axis=0, keepdims=True)
        carry = carry + total[32 * i:32 * i + 32]
        ranks.append(one_hot(ids_cap, rank))
    loads[4].wait()
    loads[2].wait()
    ids_bucket = row_ids(32, elements, 1)
    element = lax.broadcasted_iota(jnp.int32, (1, elements), 1)
    sums = None
    for k in range(slots):
        line = bucket_of[k:k + 1, :]
        hot_rank = jnp.concatenate(ranks[k * per:(k + 1) * per], axis=1)
        cells = target[0, k:k + 1, :]
        high, low = split(crossing[0, k:k + 1, :])
        parts = [
            (element & -16).astype(F32).astype(BF16), high, (cells & -256).astype(F32).astype(BF16),
            (element & 15).astype(F32).astype(BF16), low, (cells & 255).astype(F32).astype(BF16),
        ]
        left = jnp.concatenate(
            [spread(ids_bucket, line, jnp.broadcast_to(x.astype(F32), (16, elements)).astype(BF16)) for x in parts],
            axis=0)
        part = lax.dot_general(left, hot_rank, NT, preferred_element_type=F32)
        sums = part if k == 0 else sums + part
    sums = sums[:96] + sums[96:]
    for kind in range(3):
        lists[0, :, :, kind] = sums[32 * kind:32 * kind + buckets].reshape(n_ev, 3, 1, cap)
    arrive_lists((0,))

    ids_hi = row_ids(32 * 8, cap, 8)
    ids_lo = row_ids(256, cap, 1)

    def collect(q, done=None):
        hots, lines, values = [], [], []
        for s in (1, 0, 2):
            if s != 1:
                when(has[2 - s], lambda q=q, s=s: lists_sideways(q, s).wait_recv())
                when(has[2 - s], lambda q=q, s=s: sideways(q, s).wait_recv())
            listed = lists[q, q, 1] if s == 1 else side_lists[s // 2, q]
            source = jnp.concatenate([raw[2 - s, q, h] for h in range(PIECES)], axis=1)
            high = source.astype(BF16).astype(F32)
            source = jnp.concatenate([high, source - high], axis=0).astype(BF16)
            chosen = listed[0]
            pick = jnp.concatenate(
                [one_hot(ids_lo, chosen - 256.0 * i) for i in range(elements // 256)], axis=0)
            value = lax.dot_general(source, pick, NN, preferred_element_type=F32)
            values.append((value[:24] + value[24:]) * listed[1])
            cells = listed[2].astype(jnp.int32)
            hots.append(one_hot(ids_lo, (cells & 255).astype(F32)))
            lines.append((cells >> 8).astype(F32))
        right = jnp.concatenate(hots, axis=1)
        for g in range(3):
            highs, lows = [], []
            for value, line in zip(values, lines):
                high, low = split(value[8 * g:8 * g + 8])
                highs.append(spread(ids_hi, line, twice(high)))
                lows.append(spread(ids_hi, line, twice(low)))
            left = jnp.concatenate([jnp.concatenate(highs, axis=1), jnp.concatenate(lows, axis=1)], axis=0)
            part = lax.dot_general(left, right, NT, preferred_element_type=F32)
            part = (part[:256] + part[256:]).reshape(4, 4, 2, 8, 256)
            for z in range(2):
                lanes = slice(z * 256, (z + 1) * 256)
                if q == 0:
                    field[0, g, :, :, :, lanes] = part[:, :, z]
                else:
                    field[0, g, :, :, :, lanes] += part[:, :, z]
            if done is not None:
                done(g)

    faces = (
        (ev < n_ev - 1, ev > 0, (ev + 1, sp), lambda t, g: field.at[t, g, 3]),
        (ev > 0, ev < n_ev - 1, (ev - 1, sp), lambda t, g: field.at[t, g, 0]),
        (sp < n_sp - 1, sp > 0, (ev, sp + 1), lambda t, g: field.at[t, g, :, 3]),
        (sp > 0, sp < n_sp - 1, (ev, sp - 1), lambda t, g: field.at[t, g, :, 0]),
    )

    def face_copy(t, g, face):
        _, _, device, source = faces[face]
        return pltpu.make_async_remote_copy(
            src_ref=source(t, g), dst_ref=halo.at[t, face, g], send_sem=halo_out_sem.at[t, face, g],
            recv_sem=halo_in_sem.at[t, face, g], device_id=device, device_id_type=MESH)

    def send_faces(t, g):
        for face in range(4):
            when(faces[face][0], lambda face=face: face_copy(t, g, face).start())

    lane = lax.broadcasted_iota(jnp.int32, (32, 512), 1)

    def step(t, g):
        for face in range(4):
            when(faces[face][1], lambda face=face: face_copy(t, g, face).wait_recv())
        for a in range(4):
            center = field[t, g, a]
            above = halo[t, 0, g] if a == 0 else field[t, g, a - 1]
            below = halo[t, 1, g] if a == 3 else field[t, g, a + 1]
            around = above + below
            around += jnp.concatenate([halo[t, 2, g, a][None], center[:3]], axis=0)
            around += jnp.concatenate([center[1:], halo[t, 3, g, a][None]], axis=0)
            flat = center.reshape(32, 512)
            left = jnp.where(lane == 0, 0.0, pltpu.roll(flat, 1, 1))
            right = jnp.where(lane == 511, 0.0, pltpu.roll(flat, 511, 1))
            around += (left + right).reshape(4, 8, 512)
            coeff = diffusivity[a].reshape(4, 1, 512)
            new = center + coeff * (around - 6.0 * center)
            if t < STEPS - 1:
                field[t + 1, g, a] = new
            else:
                for b2 in range(4):
                    for zt in range(4):
                        rows = pl.ds(g * 512 + a * 16 + zt * 4 + b2, 8, stride=64)
                        out[rows, :] = new[b2, :, zt * 128:(zt + 1) * 128]
        if t < STEPS - 1:
            send_faces(t + 1, g)

    arrive((1, n_ev - 1))
    arrive_lists((1, n_ev - 1))
    collect(0)
    arrive((2, n_ev - 2))
    arrive_lists((2, n_ev - 2))
    collect(1)
    collect(n_ev - 1)
    arrive((3, n_ev - 3))
    arrive_lists((3, n_ev - 3))
    collect(2)
    arrive((half,))
    arrive_lists((half,))
    collect(n_ev - 2)
    collect(3)
    collect(n_ev - 3)
    collect(half, lambda g: send_faces(0, g))
    loads[5].wait()
    for t in range(STEPS):
        for g in range(3):
            step(t, g)

    for q in range(n_ev):
        for up in pass_lists_to(q):
            pass_lists(q, up).wait_send()
        for up in (True, False):
            for h in ring_pieces(q, up):
                ring(q, h, up).wait_send()
        for s in (0, 2):
            when(has[s], lambda q=q, s=s: lists_sideways(q, s).wait_send())
            when(has[s], lambda q=q, s=s: sideways(q, s).wait_send())
    for t in range(STEPS):
        for g in range(3):
            for face in range(4):
                when(faces[face][0], lambda face=face: face_copy(t, g, face).wait_send())


def solution(mesh):
    n_ev, n_sp = mesh.shape["ev"], mesh.shape["sp"]

    def per_device(*arguments):
        crossing = arguments[2]
        elements = crossing.shape[2]
        cap = crossing.shape[1] * elements // (2 * n_ev)
        arguments = [pltpu.with_memory_space_constraint(x, pltpu.HBM) for x in arguments]
        result = pl.pallas_call(
            functools.partial(kernel, n_ev, n_sp),
            out_shape=jax.ShapeDtypeStruct((1536, 128), F32),
            in_specs=[pl.BlockSpec(memory_space=pl.ANY)] * 6,
            out_specs=pl.BlockSpec(memory_space=pltpu.VMEM),
            scratch_shapes=[
                *[pltpu.VMEM(x.shape, x.dtype) for x in arguments],
                pltpu.SemaphoreType.DMA((6,)),
                pltpu.VMEM((3, n_ev, PIECES, 24, elements // PIECES), F32),
                pltpu.VMEM((n_ev, n_ev, 3, 3, 1, cap), F32),
                pltpu.VMEM((2, n_ev, 3, 1, cap), F32),
                pltpu.VMEM((STEPS, 3, 4, 4, 8, 512), F32),
                pltpu.VMEM((STEPS, 4, 3, 4, 8, 512), F32),
                pltpu.SemaphoreType.DMA((2, n_ev, PIECES)),
                pltpu.SemaphoreType.DMA((n_ev, PIECES)),
                pltpu.SemaphoreType.DMA((2, n_ev)),
                pltpu.SemaphoreType.DMA((2, n_ev)),
                pltpu.SemaphoreType.DMA((2, n_ev)),
                pltpu.SemaphoreType.DMA((n_ev,)),
                pltpu.SemaphoreType.DMA((2, n_ev)),
                pltpu.SemaphoreType.DMA((2, n_ev)),
                pltpu.SemaphoreType.DMA((STEPS, 4, 3)),
                pltpu.SemaphoreType.DMA((STEPS, 4, 3)),
            ],
            compiler_params=pltpu.CompilerParams(
                collective_id=0, has_side_effects=True, vmem_limit_bytes=40 * 1024 * 1024),
        )(*arguments)
        result = result.reshape(24, 4, 4, 4, 128).transpose(0, 1, 3, 2, 4)
        return result.reshape(24, 4, 4, 512)

    return jax.shard_map(
        per_device,
        mesh=mesh,
        in_specs=(
            P("ev", None, None, "sp"),
            P(),
            P("ev", None, "sp"),
            P("ev", None, "sp"),
            P("ev", None, "sp"),
            P("ev", "sp", None),
        ),
        out_specs=P(None, "ev", "sp", None),
        check_vma=False,
    )
```

time: 62.2 us -> 50.4 us (0.81)
  Pallas kernels: 55.6 us -> 49.5 us
  local copies, waits for them, and re-layouts: 6.16 us -> 0.88 us
    pallas_call x1, Pallas kernels: 55.6 us -> 49.5 us  [per_device(): pl.pallas_call(functools.partial(kernel, n_ev, n_sp), out_shape=jax.Shape...]
    unnamed x12 -> x1, local copies, waits for them, and re-layouts: 4.72 us -> 0.88 us
    reshape x2 -> x0, local copies, waits for them, and re-layouts: 1.44 us -> none  [per_device(): return result.reshape(24, 4, 4, 512)]
where the time goes in v2:
time: 50.4 us; the launch traced here: 50.3 us
  Pallas kernels  49.5 us (98%)
  local copies, waits for them, and re-layouts  0.88 us (2%)
    pallas_call x1, Pallas kernels, per_device(): pl.pallas_call(functools.partial(kernel, n_ev, n_sp), out_shape=jax.Shape...  49.5 us

profile of v2, /device:TPU:6, one launch (start us, length us, event | category | flops | bytes accessed | tf_op | source)
XLA Modules:
  0.0 50.3 jit_solution(14059100328834853821)
XLA Ops:
  0.0 49.5 %shard_map.64 = f32[1536,128]{1,0:T(8,128)S(1)} custom-call(bf16[1,3,125,1024]{3,2,1,0:T(8,128)(2,1)} %refs_0_.1, bf16[8,125]{1,0:T(8,128)(2,1)} %refs_1_.1, f32[1,4,1024]{2,1,0:T(4,128)} %refs_2_.1, s32[1,4,1024]{2,1,0:T(4,128)} %refs_3_.1, s32[1,4,1024]{2,1,0:T(4,128)} %refs_4_.1, f32[4,4,512]{2,1,0:T(4,128)} %refs_5_.1), custom_call_target="tpu_custom_call" | custom-call | tf_op jit(solution)/shard_map/pallas_call | solution.py:348
  49.5 0.9 %copy.9 = f32[24,4,4,512]{3,2,1,0:T(4,128)} copy(f32[24,4,4,512]{3,2,1,0:T(4,128)S(1)} %bitcast.5) | data formatting | bytes 1572864

commit v3 on v1

v3 whole, which is shorter than its diff:
```python
import jax
import jax.numpy as jnp
from jax import lax
from jax.experimental import pallas as pl
from jax.experimental.pallas import tpu as pltpu
from jax.sharding import PartitionSpec as P

MESH = pl.DeviceIdType.MESH
STEPS = 4
F32 = jnp.float32
BF16 = jnp.bfloat16
NT = (((1,), (1,)), ((), ()))


def split(value):
    high = value.astype(BF16)
    low = (value - high.astype(F32)).astype(BF16)
    return high, low


def row_ids(rows, columns, group):
    return (lax.broadcasted_iota(jnp.int32, (rows, columns), 0) // group).astype(F32).astype(BF16)


def spread(ids, row, values):
    repeats = ids.shape[0] // values.shape[0]
    wide = jnp.broadcast_to(row.astype(BF16), ids.shape)
    tiled = jnp.concatenate([values] * repeats, axis=0)
    return jnp.where(ids == wide, tiled, jnp.zeros_like(tiled))


def kernel(n_ev, n_sp, *refs):
    sources, out, inputs, input_sem = refs[:6], refs[6], refs[7:13], refs[13]
    loads = [pltpu.make_async_copy(sources[i], inputs[i], input_sem.at[i]) for i in range(6)]
    for i in (3, 4, 0, 1, 2, 5):
        loads[i].start()
    body(n_ev, n_sp, loads, *inputs, out, *refs[14:])


def body(n_ev, n_sp, loads, kernels, basis, crossing, owner, target, diffusivity, out,
           value_send, cell_send, value_recv, cell_recv, field, halo, hot_lo,
           value_out_sem, cell_out_sem, value_in_sem, cell_in_sem, halo_out_sem, halo_in_sem):
    ev = lax.axis_index("ev")
    sp = lax.axis_index("sp")
    buckets = 3 * n_ev
    slots, elements = crossing.shape[1], crossing.shape[2]
    cap = value_send.shape[3]
    has = {0: sp > 0, 1: None, 2: sp < n_sp - 1}

    def when(condition, body):
        if condition is None:
            body()
        else:
            pl.when(condition)(body)

    def peer(bucket):
        return (lax.rem(ev + bucket // 3, n_ev), sp + bucket % 3 - 1)

    barrier = pltpu.get_barrier_semaphore()
    for bucket in range(buckets):
        if bucket == 1:
            continue

        def greet(bucket=bucket):
            pl.semaphore_signal(barrier, inc=1, device_id=peer(bucket), device_id_type=MESH)
        when(has[bucket % 3], greet)

    for side, missing in ((2, sp == 0), (0, sp == n_sp - 1)):
        @pl.when(missing)
        def _(side=side):
            for q in range(n_ev):
                value_recv[:, 3 * q + side] = jnp.zeros((3,) + value_recv.shape[2:], F32)
                cell_recv[3 * q + side] = jnp.zeros(cell_recv.shape[1:], F32)
    for face, missing in enumerate((ev == 0, ev == n_ev - 1, sp == 0, sp == n_sp - 1)):
        @pl.when(missing)
        def _(face=face):
            for t in range(STEPS):
                halo[t, face] = jnp.zeros(halo.shape[2:], F32)

    loads[3].wait()
    owners = owner[0]
    row = lax.rem((owners >> 5) - ev + n_ev, n_ev)
    side = (owners & (n_sp - 1)) - sp + 1
    bucket_of = (row * 3 + side).astype(F32)
    chunk = 256
    per = elements // chunk
    ids32 = lax.broadcasted_iota(jnp.int32, (32, chunk), 0).astype(F32)
    hots = []
    for k in range(slots):
        for h in range(per):
            line = bucket_of[k:k + 1, h * chunk:(h + 1) * chunk]
            hots.append(jnp.where(ids32 == line, 1.0, 0.0))
    hot = jnp.concatenate(hots, axis=0).astype(BF16)
    ri = lax.broadcasted_iota(jnp.int32, (chunk, chunk), 0)
    ci = lax.broadcasted_iota(jnp.int32, (chunk, chunk), 1)
    before = jnp.where(ri < ci, 1.0, 0.0).astype(BF16)
    prefix = jnp.dot(hot, before, preferred_element_type=F32)
    total = jnp.dot(hot, jnp.ones((chunk, chunk), BF16), preferred_element_type=F32)
    carry = jnp.zeros((32, chunk), F32)
    rank_ids = row_ids(cap, chunk, 1)
    ranks = []
    for i in range(slots * per):
        rank = jnp.sum(hots[i] * (prefix[32 * i:32 * i + 32] + carry), axis=0, keepdims=True)
        carry = carry + total[32 * i:32 * i + 32]
        wide = jnp.broadcast_to(rank.astype(BF16), rank_ids.shape)
        ranks.append(jnp.where(rank_ids == wide, jnp.ones_like(wide), jnp.zeros_like(wide)))
    def bucket(group):
        total = None
        for k in range(slots):
            line = bucket_of[k:k + 1, :]
            hot_rank = jnp.concatenate(ranks[k * per:(k + 1) * per], axis=1)
            if group is None:
                cells = target[0, k:k + 1, :]
                high = jnp.broadcast_to((cells & -256).astype(F32).astype(BF16), (16, elements))
                low = jnp.broadcast_to((cells & 255).astype(F32).astype(BF16), (16, elements))
                ids = row_ids(32, elements, 1)
            else:
                high, low = split(projected[group] * crossing[0, k:k + 1, :])
                high = jnp.concatenate([high, high], axis=0)
                low = jnp.concatenate([low, low], axis=0)
                ids = row_ids(buckets * 8, elements, 8)
            left = jnp.concatenate([spread(ids, line, high), spread(ids, line, low)], axis=0)
            part = lax.dot_general(left, hot_rank, NT, preferred_element_type=F32)
            total = part if k == 0 else total + part
        total = total[:total.shape[0] // 2] + total[total.shape[0] // 2:]
        if group is None:
            cell_send[...] = total[:buckets].reshape(buckets, 1, cap)
        else:
            value_send[group] = total.reshape(buckets, 8, cap)

    def move(bucket, group):
        source, dest, out_sem, in_sem = (
            (cell_send, cell_recv, cell_out_sem, cell_in_sem) if group is None else
            (value_send.at[group], value_recv.at[group], value_out_sem.at[group], value_in_sem.at[group]))
        return pltpu.make_async_remote_copy(
            src_ref=source.at[bucket], dst_ref=dest.at[bucket], send_sem=out_sem.at[bucket],
            recv_sem=in_sem.at[bucket], device_id=peer(bucket), device_id_type=MESH)

    order = [0] + [q for d in range(1, n_ev // 2) for q in (d, n_ev - d)] + [n_ev // 2]

    def send(group):
        for q in order:
            for s in range(3):
                if 3 * q + s != 1:
                    when(has[s], lambda b=3 * q + s: move(b, group).start())
        if group is None:
            cell_recv[1] = cell_send[1]
        else:
            value_recv[group, 1] = value_send[group, 1]

    for i in (0, 1, 2):
        loads[i].wait()
    projected = [
        lax.dot_general(basis[...], kernels[0, p], (((1,), (0,)), ((), ())), preferred_element_type=F32)
        for p in range(kernels.shape[1])
    ]

    def sent(group):
        for b in range(buckets):
            if b != 1:
                when(has[b % 3], lambda b=b: move(b, group).wait_send())

    bucket(0)
    pl.semaphore_wait(barrier, n_ev - 1 + n_ev * ((sp > 0).astype(jnp.int32) + (sp < n_sp - 1).astype(jnp.int32)))
    send(0)
    loads[4].wait()
    bucket(None)
    send(None)
    loads[5].wait()

    ids_hi = row_ids(32 * 8, cap, 8)
    ids_lo = row_ids(256, cap, 1)

    def scatter(group):
        field[0, group] = jnp.zeros(field.shape[2:], F32)
        for q in order:
            highs, lows = [], []
            for s in range(3):
                b = 3 * q + s
                if b != 1:
                    when(has[2 - s], lambda b=b: move(b, group).wait_recv())
                    if group == 0:
                        when(has[2 - s], lambda b=b: move(b, None).wait_recv())
                cells = cell_recv[b].astype(jnp.int32)
                if group == 0:
                    wide = jnp.broadcast_to((cells & 255).astype(F32).astype(BF16), ids_lo.shape)
                    hot_lo[q, :, s * cap:(s + 1) * cap] = jnp.where(
                        ids_lo == wide, jnp.ones_like(wide), jnp.zeros_like(wide))
                line = (cells >> 8).astype(F32)
                high, low = split(value_recv[group, b])
                high = jnp.concatenate([high, high], axis=0)
                low = jnp.concatenate([low, low], axis=0)
                highs.append(spread(ids_hi, line, high))
                lows.append(spread(ids_hi, line, low))
            right = hot_lo[q]
            left = jnp.concatenate(highs + lows, axis=1)
            part = lax.dot_general(left, jnp.concatenate([right, right], axis=1), NT, preferred_element_type=F32)
            part = part.reshape(4, 4, 2, 8, 256)
            for z in range(2):
                field[0, group, :, :, :, z * 256:(z + 1) * 256] += part[:, :, z]

    faces = (
        (ev < n_ev - 1, ev > 0, (ev + 1, sp), lambda t, g: field.at[t, g, 3]),
        (ev > 0, ev < n_ev - 1, (ev - 1, sp), lambda t, g: field.at[t, g, 0]),
        (sp < n_sp - 1, sp > 0, (ev, sp + 1), lambda t, g: field.at[t, g, :, 3]),
        (sp > 0, sp < n_sp - 1, (ev, sp - 1), lambda t, g: field.at[t, g, :, 0]),
    )
    def face_copy(t, g, face):
        _, _, device, source = faces[face]
        return pltpu.make_async_remote_copy(
            src_ref=source(t, g), dst_ref=halo.at[t, face, g], send_sem=halo_out_sem.at[t, face, g],
            recv_sem=halo_in_sem.at[t, face, g], device_id=device, device_id_type=MESH)

    def send_faces(t, g, which=range(4)):
        for face in which:
            when(faces[face][0], lambda face=face: face_copy(t, g, face).start())

    lane = lax.broadcasted_iota(jnp.int32, (32, 512), 1)
    def step(t, g):
        for face in range(4):
            when(faces[face][1], lambda face=face: face_copy(t, g, face).wait_recv())
        for a in (0, 3, 1, 2):
            center = field[t, g, a]
            above = halo[t, 0, g] if a == 0 else field[t, g, a - 1]
            below = halo[t, 1, g] if a == 3 else field[t, g, a + 1]
            around = above + below
            around += jnp.concatenate([halo[t, 2, g, a][None], center[:3]], axis=0)
            around += jnp.concatenate([center[1:], halo[t, 3, g, a][None]], axis=0)
            flat = center.reshape(32, 512)
            left = jnp.where(lane == 0, 0.0, pltpu.roll(flat, 1, 1))
            right = jnp.where(lane == 511, 0.0, pltpu.roll(flat, 511, 1))
            around += (left + right).reshape(4, 8, 512)
            coeff = diffusivity[a].reshape(4, 1, 512)
            new = center + coeff * (around - 6.0 * center)
            if t < STEPS - 1:
                field[t + 1, g, a] = new
                if a in (0, 3):
                    send_faces(t + 1, g, (1 if a == 0 else 0,))
            else:
                for b2 in range(4):
                    for zt in range(4):
                        out[pl.ds(g * 512 + a * 16 + zt * 4 + b2, 8, stride=64), :] = new[b2, :, zt * 128:(zt + 1) * 128]
        if t < STEPS - 1:
            send_faces(t + 1, g, (2, 3))

    bucket(1)
    bucket(2)
    sent(0)
    send(1)
    send(2)
    scatter(0)
    send_faces(0, 0)
    scatter(1)
    send_faces(0, 1)
    scatter(2)
    send_faces(0, 2)
    for t in range(STEPS):
        for g in range(3):
            step(t, g)

    for group in (None, 1, 2,):
        sent(group)
    for t in range(STEPS):
        for g in range(3):
            for face in range(4):
                when(faces[face][0], lambda face=face: face_copy(t, g, face).wait_send())


def solution(mesh):
    n_ev, n_sp = mesh.shape["ev"], mesh.shape["sp"]

    def per_device(kernels, basis, crossing, owner, target, diffusivity):
        import functools
        buckets = 3 * n_ev
        cap = crossing.shape[1] * crossing.shape[2] // (2 * n_ev)
        arguments = [pltpu.with_memory_space_constraint(x, pltpu.HBM) for x in (kernels, basis, crossing, owner, target, diffusivity)]
        result = pl.pallas_call(
            functools.partial(kernel, n_ev, n_sp),
            out_shape=jax.ShapeDtypeStruct((1536, 128), F32),
            in_specs=[pl.BlockSpec(memory_space=pl.ANY)] * 6,
            out_specs=pl.BlockSpec(memory_space=pltpu.VMEM),
            scratch_shapes=[
                *[pltpu.VMEM(x.shape, x.dtype) for x in arguments],
                pltpu.SemaphoreType.DMA((6,)),
                pltpu.VMEM((3, buckets, 8, cap), F32),
                pltpu.VMEM((buckets, 1, cap), F32),
                pltpu.VMEM((3, buckets, 8, cap), F32),
                pltpu.VMEM((buckets, 1, cap), F32),
                pltpu.VMEM((STEPS, 3, 4, 4, 8, 512), F32),
                pltpu.VMEM((STEPS, 4, 3, 4, 8, 512), F32),
                pltpu.VMEM((n_ev, 256, 3 * cap), BF16),
                pltpu.SemaphoreType.DMA((3, buckets)),
                pltpu.SemaphoreType.DMA((buckets,)),
                pltpu.SemaphoreType.DMA((3, buckets)),
                pltpu.SemaphoreType.DMA((buckets,)),
                pltpu.SemaphoreType.DMA((STEPS, 4, 3)),
                pltpu.SemaphoreType.DMA((STEPS, 4, 3)),
            ],
            compiler_params=pltpu.CompilerParams(
                collective_id=0, has_side_effects=True, vmem_limit_bytes=40 * 1024 * 1024),
        )(*arguments)
        result = result.reshape(24, 4, 4, 4, 128).transpose(0, 1, 3, 2, 4)
        return result.reshape(24, 4, 4, 512)

    return jax.shard_map(
        per_device,
        mesh=mesh,
        in_specs=(
            P("ev", None, None, "sp"),
            P(),
            P("ev", None, "sp"),
            P("ev", None, "sp"),
            P("ev", None, "sp"),
            P("ev", "sp", None),
        ),
        out_specs=P(None, "ev", "sp", None),
        check_vma=False,
    )
```

time: 62.2 us -> 49.3 us (0.79)
  Pallas kernels: 55.6 us -> 47.7 us
  local copies, waits for them, and re-layouts: 6.16 us -> 0.88 us
    pallas_call x1, Pallas kernels: 55.6 us -> 47.7 us  [per_device(): pl.pallas_call(functools.partial(kernel, n_ev, n_sp), out_shape=jax.Shape...]
    unnamed x12 -> x1, local copies, waits for them, and re-layouts: 4.72 us -> 0.88 us
    reshape x2 -> x0, local copies, waits for them, and re-layouts: 1.44 us -> none  [per_device(): return result.reshape(24, 4, 4, 512)]
where the time goes in v3:
time: 49.3 us; the launch traced here: 48.6 us
  Pallas kernels  47.7 us (97%)
  local copies, waits for them, and re-layouts  0.88 us (2%)
    pallas_call x1, Pallas kernels, per_device(): pl.pallas_call(functools.partial(kernel, n_ev, n_sp), out_shape=jax.Shape...  47.7 us

profile of v3, /device:TPU:6, one launch (start us, length us, event | category | flops | bytes accessed | tf_op | source)
XLA Modules:
  0.0 48.6 jit_solution(13552366675939030533)
XLA Ops:
  0.0 47.7 %shard_map.64 = f32[1536,128]{1,0:T(8,128)S(1)} custom-call(bf16[1,3,125,1024]{3,2,1,0:T(8,128)(2,1)} %refs_0_.1, bf16[8,125]{1,0:T(8,128)(2,1)} %refs_1_.1, f32[1,4,1024]{2,1,0:T(4,128)} %refs_2_.1, s32[1,4,1024]{2,1,0:T(4,128)} %refs_3_.1, s32[1,4,1024]{2,1,0:T(4,128)} %refs_4_.1, f32[4,4,512]{2,1,0:T(4,128)} %refs_5_.1), custom_call_target="tpu_custom_call" | custom-call | tf_op jit(solution)/shard_map/pallas_call | solution.py:277
  47.7 0.9 %copy.9 = f32[24,4,4,512]{3,2,1,0:T(4,128)} copy(f32[24,4,4,512]{3,2,1,0:T(4,128)S(1)} %bitcast.5) | data formatting | bytes 1572864

commit v4 on v3

--- a/solution.py
+++ b/solution.py
@@ -31,8 +31,9 @@
 
 def kernel(n_ev, n_sp, *refs):
     sources, out, inputs, input_sem = refs[:6], refs[6], refs[7:13], refs[13]
-    loads = [pltpu.make_async_copy(sources[i], inputs[i], input_sem.at[i]) for i in range(6)]
-    for i in (3, 4, 0, 1, 2, 5):
+    loads = [pltpu.make_async_copy(sources[i], inputs[i], input_sem.at[i]) for i in range(1, 6)]
+    loads += [pltpu.make_async_copy(sources[0].at[:, p], inputs[0].at[:, p], input_sem.at[6 + p]) for p in range(3)]
+    for i in (2, 0, 5, 1, 6, 7, 3, 4):
         loads[i].start()
     body(n_ev, n_sp, loads, *inputs, out, *refs[14:])
 
@@ -53,17 +54,26 @@
         else:
             pl.when(condition)(body)
 
+    inside = jnp.logical_and(sp > 0, sp < n_sp - 1)
+
+    def each(pairs, act):
+        @pl.when(inside)
+        def _():
+            for q, s in pairs:
+                act(q, s)
+
+        @pl.when(jnp.logical_not(inside))
+        def _():
+            for q, s in pairs:
+                when(has[s], lambda q=q, s=s: act(q, s))
+
     def peer(bucket):
         return (lax.rem(ev + bucket // 3, n_ev), sp + bucket % 3 - 1)
 
     barrier = pltpu.get_barrier_semaphore()
-    for bucket in range(buckets):
-        if bucket == 1:
-            continue
-
-        def greet(bucket=bucket):
-            pl.semaphore_signal(barrier, inc=1, device_id=peer(bucket), device_id_type=MESH)
-        when(has[bucket % 3], greet)
+    distant = [half for d in range(1, n_ev // 2) for half in (n_ev - d, d)]
+    each([(q, s) for q in [n_ev // 2] + distant[::-1] + [0] for s in range(3) if 3 * q + s != 1], lambda q, s: pl.semaphore_signal(
+        barrier, inc=1, device_id=peer(3 * q + s), device_id_type=MESH))
 
     for side, missing in ((2, sp == 0), (0, sp == n_sp - 1)):
         @pl.when(missing)
@@ -77,7 +87,7 @@
             for t in range(STEPS):
                 halo[t, face] = jnp.zeros(halo.shape[2:], F32)
 
-    loads[3].wait()
+    loads[2].wait()
     owners = owner[0]
     row = lax.rem((owners >> 5) - ev + n_ev, n_ev)
     side = (owners & (n_sp - 1)) - sp + 1
@@ -139,34 +149,29 @@
     order = [0] + [q for d in range(1, n_ev // 2) for q in (d, n_ev - d)] + [n_ev // 2]
 
     def send(group):
-        for q in order:
-            for s in range(3):
-                if 3 * q + s != 1:
-                    when(has[s], lambda b=3 * q + s: move(b, group).start())
+        each([(q, s) for q in order for s in range(3) if 3 * q + s != 1], lambda q, s: move(3 * q + s, group).start())
         if group is None:
             cell_recv[1] = cell_send[1]
         else:
             value_recv[group, 1] = value_send[group, 1]
 
-    for i in (0, 1, 2):
-        loads[i].wait()
-    projected = [
-        lax.dot_general(basis[...], kernels[0, p], (((1,), (0,)), ((), ())), preferred_element_type=F32)
-        for p in range(kernels.shape[1])
-    ]
+    def project(p):
+        loads[5 + p].wait()
+        return lax.dot_general(basis[...], kernels[0, p], (((1,), (0,)), ((), ())), preferred_element_type=F32)
 
     def sent(group):
-        for b in range(buckets):
-            if b != 1:
-                when(has[b % 3], lambda b=b: move(b, group).wait_send())
-
+        each([(q, s) for q in order for s in range(3) if 3 * q + s != 1], lambda q, s: move(3 * q + s, group).wait_send())
+
+    loads[0].wait()
+    loads[1].wait()
+    projected = [project(0)]
     bucket(0)
     pl.semaphore_wait(barrier, n_ev - 1 + n_ev * ((sp > 0).astype(jnp.int32) + (sp < n_sp - 1).astype(jnp.int32)))
     send(0)
-    loads[4].wait()
+    loads[3].wait()
     bucket(None)
     send(None)
-    loads[5].wait()
+    loads[4].wait()
 
     ids_hi = row_ids(32 * 8, cap, 8)
     ids_lo = row_ids(256, cap, 1)
@@ -215,6 +220,10 @@
         for face in which:
             when(faces[face][0], lambda face=face: face_copy(t, g, face).start())
 
+    def faces_sent(t, g):
+        for face in range(4):
+            when(faces[face][0], lambda face=face: face_copy(t, g, face).wait_send())
+
     lane = lax.broadcasted_iota(jnp.int32, (32, 512), 1)
     def step(t, g):
         for face in range(4):
@@ -243,6 +252,7 @@
         if t < STEPS - 1:
             send_faces(t + 1, g, (2, 3))
 
+    projected += [project(1), project(2)]
     bucket(1)
     bucket(2)
     sent(0)
@@ -254,16 +264,16 @@
     send_faces(0, 1)
     scatter(2)
     send_faces(0, 2)
+    for group in (None, 1, 2):
+        sent(group)
     for t in range(STEPS):
         for g in range(3):
             step(t, g)
-
-    for group in (None, 1, 2,):
-        sent(group)
-    for t in range(STEPS):
-        for g in range(3):
-            for face in range(4):
-                when(faces[face][0], lambda face=face: face_copy(t, g, face).wait_send())
+            if t > 0:
+                faces_sent(t - 1, g)
+
+    for g in range(3):
+        faces_sent(STEPS - 1, g)
 
 
 def solution(mesh):
@@ -281,7 +291,7 @@
             out_specs=pl.BlockSpec(memory_space=pltpu.VMEM),
             scratch_shapes=[
                 *[pltpu.VMEM(x.shape, x.dtype) for x in arguments],
-                pltpu.SemaphoreType.DMA((6,)),
+                pltpu.SemaphoreType.DMA((9,)),
                 pltpu.VMEM((3, buckets, 8, cap), F32),
                 pltpu.VMEM((buckets, 1, cap), F32),
                 pltpu.VMEM((3, buckets, 8, cap), F32),

time: 49.3 us -> 49 us (level)
  no operation moved by 1% of the time
where the time goes in v4:
time: 49 us; the launch traced here: 48.6 us
  Pallas kernels  47.7 us (97%)
  local copies, waits for them, and re-layouts  0.88 us (2%)
    pallas_call x1, Pallas kernels, per_device(): pl.pallas_call(functools.partial(kernel, n_ev, n_sp), out_shape=jax.Shape...  47.7 us

profile of v4, /device:TPU:6, one launch (start us, length us, event | category | flops | bytes accessed | tf_op | source)
XLA Modules:
  0.0 48.6 jit_solution(11690457370797547374)
XLA Ops:
  0.0 47.7 %shard_map.64 = f32[1536,128]{1,0:T(8,128)S(1)} custom-call(bf16[1,3,125,1024]{3,2,1,0:T(8,128)(2,1)} %refs_0_.1, bf16[8,125]{1,0:T(8,128)(2,1)} %refs_1_.1, f32[1,4,1024]{2,1,0:T(4,128)} %refs_2_.1, s32[1,4,1024]{2,1,0:T(4,128)} %refs_3_.1, s32[1,4,1024]{2,1,0:T(4,128)} %refs_4_.1, f32[4,4,512]{2,1,0:T(4,128)} %refs_5_.1), custom_call_target="tpu_custom_call" | custom-call | tf_op jit(solution)/shard_map/pallas_call | solution.py:287
  47.7 0.9 %copy.9 = f32[24,4,4,512]{3,2,1,0:T(4,128)} copy(f32[24,4,4,512]{3,2,1,0:T(4,128)S(1)} %bitcast.5) | data formatting | bytes 1572864

commit v5 on v4

--- a/solution.py
+++ b/solution.py
@@ -159,8 +159,8 @@
         loads[5 + p].wait()
         return lax.dot_general(basis[...], kernels[0, p], (((1,), (0,)), ((), ())), preferred_element_type=F32)
 
-    def sent(group):
-        each([(q, s) for q in order for s in range(3) if 3 * q + s != 1], lambda q, s: move(3 * q + s, group).wait_send())
+    def sent(group, rows=order):
+        each([(q, s) for q in rows for s in range(3) if 3 * q + s != 1], lambda q, s: move(3 * q + s, group).wait_send())
 
     loads[0].wait()
     loads[1].wait()
@@ -255,7 +255,7 @@
     projected += [project(1), project(2)]
     bucket(1)
     bucket(2)
-    sent(0)
+    sent(0, order[:5])
     send(1)
     send(2)
     scatter(0)
@@ -264,6 +264,7 @@
     send_faces(0, 1)
     scatter(2)
     send_faces(0, 2)
+    sent(0, order[5:])
     for group in (None, 1, 2):
         sent(group)
     for t in range(STEPS):

time: 49 us -> 49 us (level)
  no operation moved by 1% of the time
where the time goes in v5:
time: 49 us; the launch traced here: 48.6 us
  Pallas kernels  47.7 us (97%)
  local copies, waits for them, and re-layouts  0.88 us (2%)
    pallas_call x1, Pallas kernels, per_device(): pl.pallas_call(functools.partial(kernel, n_ev, n_sp), out_shape=jax.Shape...  47.7 us

profile of v5, /device:TPU:6, one launch (start us, length us, event | category | flops | bytes accessed | tf_op | source)
XLA Modules:
  0.0 48.6 jit_solution(5525491604518339735)
XLA Ops:
  0.0 47.7 %shard_map.64 = f32[1536,128]{1,0:T(8,128)S(1)} custom-call(bf16[1,3,125,1024]{3,2,1,0:T(8,128)(2,1)} %refs_0_.1, bf16[8,125]{1,0:T(8,128)(2,1)} %refs_1_.1, f32[1,4,1024]{2,1,0:T(4,128)} %refs_2_.1, s32[1,4,1024]{2,1,0:T(4,128)} %refs_3_.1, s32[1,4,1024]{2,1,0:T(4,128)} %refs_4_.1, f32[4,4,512]{2,1,0:T(4,128)} %refs_5_.1), custom_call_target="tpu_custom_call" | custom-call | tf_op jit(solution)/shard_map/pallas_call | solution.py:288
  47.7 0.9 %copy.9 = f32[24,4,4,512]{3,2,1,0:T(4,128)} copy(f32[24,4,4,512]{3,2,1,0:T(4,128)S(1)} %bitcast.5) | data formatting | bytes 1572864
